TPU v7x, 32 devices: a whole 2x2x4 slice. The times are simulated.
32 devices in a mesh: dp: 2 (over y), expert: 16 (over z, x, core).
Axes of the slice: x: 2, y: 2, z: 4, core: 2. Of those that a mesh axis runs over, the one named last changes fastest.
Arguments:
- tokens: bfloat16 [2, 512, 3584], P(None, ('dp', 'expert')), may hold values from -6 to 6
- out_grad: bfloat16 [2, 512, 3584], P(None, ('dp', 'expert')), may hold values from -6 to 6
- expert_ids: int32 [2, 512, 4], P(None, ('dp', 'expert')), may hold values from 0 to 7, all different within a row
- route_probs: float32 [2, 512, 4], P(None, ('dp', 'expert')), may hold values from 0.1 to 0.6
- copy_marks: int32 [2, 8], replicated, may hold values from 0 to 1, as said below
- w_gate: bfloat16 [3584, 8192], P(None, 'expert'), may hold values from -0.09375 to 0.09375
- w_up: bfloat16 [3584, 8192], P(None, 'expert'), may hold values from -0.09375 to 0.09375
- w_down: bfloat16 [3584, 8192], P(None, 'expert'), may hold values from -0.1875 to 0.1875
Outputs:
- moe_out: bfloat16 [2, 512, 3584], P(None, ('dp', 'expert'))
- input_grad: bfloat16 [2, 512, 3584], P(None, ('dp', 'expert'))
- grad_gate: float32 [3584, 8192], P('dp', 'expert')
- grad_up: float32 [3584, 8192], P('dp', 'expert')
- grad_down: float32 [3584, 8192], P('dp', 'expert')
Inputs may be any that keep to these rules, and one draw needn't show every extreme that they name: `copy_marks`: each row has exactly 4 ones.
All inputs are finite; a program needn't handle non-finite values.
Results may differ from a plain program's by a relative error of at most 0.0064.
Values may be sent and summed in bfloat16 or wider, within the bound.
A program may use at most 128 MiB of HBM per device.

v0:
```python
import jax
import jax.numpy as jnp
from jax import lax
from jax.sharding import PartitionSpec as P

SPLIT = 2


def slot_table(expert_ids, marks, half, experts, capacity):
    tok_rows, topk = expert_ids.shape
    flat = expert_ids.reshape(tok_rows * topk)
    labels = jnp.arange(experts, dtype=jnp.int32)
    onehot = (flat[:, None] == labels[None, :]).astype(jnp.int32)
    earlier = jnp.cumsum(onehot, axis=0) - onehot
    ranked = jnp.sum(earlier * onehot, axis=1)
    marked = jnp.sum(onehot * marks[None, :], axis=1)
    at_home = ranked < capacity
    spilled = (marked > 0) & (ranked >= capacity) & (ranked < 2 * capacity)
    target = jnp.where(at_home, half, 1 - half)
    within = jnp.where(at_home, ranked, ranked - capacity)
    placed = jnp.where(at_home | spilled, (target * experts + flat) * capacity + within, -1)
    places = 2 * experts * capacity
    table = jnp.arange(places, dtype=jnp.int32)[:, None] == placed[None, :]
    return table.reshape(places, tok_rows, topk)


def pack_rows(table, tokens_now, probs_now, cot_now, n_dp, n_ep, experts, capacity):
    places, tok_rows, topk = table.shape
    width = tokens_now.shape[1]
    picked = jnp.sum(table.astype(jnp.int32), axis=2).astype(jnp.bfloat16)
    moved = jnp.dot(picked, tokens_now, preferred_element_type=jnp.float32).astype(jnp.bfloat16)
    scaled = (probs_now[:, :, None] * cot_now[:, None, :].astype(jnp.float32)).astype(jnp.bfloat16)
    spread = jnp.dot(
        table.astype(jnp.bfloat16).reshape(places, tok_rows * topk),
        scaled.reshape(tok_rows * topk, width),
        preferred_element_type=jnp.float32,
    ).astype(jnp.bfloat16)

    def widen(block):
        shaped = block.reshape(n_dp, experts, 1, capacity, width)
        wide = jnp.broadcast_to(shaped, (n_dp, experts, n_ep // experts, capacity, width))
        return wide.reshape(n_dp * n_ep, capacity, width)

    return (widen(moved), widen(spread))


def unpack_rows(table, probs_now, back_out, back_dx, n_dp, experts, capacity):
    places = table.shape[0]
    width = back_out.shape[2]

    def fold(block):
        shaped = block.reshape(n_dp, experts, -1, capacity, width).astype(jnp.float32)
        return jnp.sum(shaped, axis=2).reshape(places, width)

    table_f = table.astype(jnp.float32)
    mixing = jnp.einsum("ptk,tk->pt", table_f, probs_now, precision=lax.Precision.HIGHEST)
    picked = jnp.sum(table_f, axis=2)
    rows_first = (((0,), (0,)), ((), ()))
    moe = lax.dot_general(
        mixing,
        fold(back_out),
        rows_first,
        precision=lax.Precision.HIGHEST,
        preferred_element_type=jnp.float32,
    )
    grad_in = lax.dot_general(
        picked,
        fold(back_dx),
        rows_first,
        precision=lax.Precision.HIGHEST,
        preferred_element_type=jnp.float32,
    )
    return (moe.astype(jnp.bfloat16), grad_in.astype(jnp.bfloat16))


def expert_pass(rows_in, scaled, w_gate, w_up, w_down):
    contract = (((1,), (1,)), ((), ()))
    rows_first = (((0,), (0,)), ((), ()))
    gate_pre = jnp.dot(rows_in, w_gate, preferred_element_type=jnp.float32)
    up_pre = jnp.dot(rows_in, w_up, preferred_element_type=jnp.float32)
    squash = jax.nn.sigmoid(gate_pre)
    active = gate_pre * squash
    hidden = (active * up_pre).astype(jnp.bfloat16)
    part_out = lax.dot_general(hidden, w_down, contract, preferred_element_type=jnp.float32).astype(
        jnp.bfloat16
    )
    down_term = lax.dot_general(scaled, hidden, rows_first, preferred_element_type=jnp.float32)
    hidden_grad = jnp.dot(scaled, w_down, preferred_element_type=jnp.float32)
    gate_grad = (hidden_grad * up_pre * squash * (1.0 + gate_pre * (1.0 - squash))).astype(
        jnp.bfloat16
    )
    up_grad = (hidden_grad * active).astype(jnp.bfloat16)
    gate_term = lax.dot_general(rows_in, gate_grad, rows_first, preferred_element_type=jnp.float32)
    up_term = lax.dot_general(rows_in, up_grad, rows_first, preferred_element_type=jnp.float32)
    part_dx = lax.dot_general(gate_grad, w_gate, contract, preferred_element_type=jnp.float32)
    part_dx = (
        part_dx + lax.dot_general(up_grad, w_up, contract, preferred_element_type=jnp.float32)
    ).astype(jnp.bfloat16)
    return (part_out, part_dx, gate_term, up_term, down_term)


def send_out(moved, spread):
    return (
        lax.all_to_all(moved, ("dp", "expert"), split_axis=0, concat_axis=0, tiled=True),
        lax.all_to_all(spread, ("dp", "expert"), split_axis=0, concat_axis=0, tiled=True),
    )


def send_back(part_out, part_dx):
    return (
        lax.all_to_all(part_out, ("dp", "expert"), split_axis=0, concat_axis=0, tiled=True),
        lax.all_to_all(part_dx, ("dp", "expert"), split_axis=0, concat_axis=0, tiled=True),
    )


def local(tokens, out_grad, expert_ids, route_probs, copy_marks, w_gate, w_up, w_down):
    n_dp = lax.axis_size("dp")
    n_ep = lax.axis_size("expert")
    experts = n_ep // SPLIT
    tok_rows, topk = (expert_ids.shape[1], expert_ids.shape[2])
    width = tokens.shape[2]
    capacity = max(1, tok_rows * topk // experts)
    devices = n_dp * n_ep
    half = lax.axis_index("dp")
    tables = [
        slot_table(expert_ids[micro], copy_marks[micro], half, experts, capacity)
        for micro in range(2)
    ]
    packed = [
        pack_rows(
            tables[micro],
            tokens[micro],
            route_probs[micro],
            out_grad[micro],
            n_dp,
            n_ep,
            experts,
            capacity,
        )
        for micro in range(2)
    ]
    moved = jnp.concatenate([packed[0][0], packed[1][0]], axis=1)
    spread = jnp.concatenate([packed[0][1], packed[1][1]], axis=1)
    got_in, got_cot = send_out(moved, spread)
    part_out, part_dx, gate_sum, up_sum, down_sum = expert_pass(
        got_in.reshape(-1, width), got_cot.reshape(-1, width), w_gate, w_up, w_down
    )
    back_out, back_dx = send_back(
        part_out.reshape(devices, 2 * capacity, width),
        part_dx.reshape(devices, 2 * capacity, width),
    )
    returned = [
        (back_out[:, :capacity], back_dx[:, :capacity]),
        (back_out[:, capacity:], back_dx[:, capacity:]),
    ]
    outputs = []
    grads_in = []
    for micro in range(2):
        moe, grad_in = unpack_rows(
            tables[micro],
            route_probs[micro],
            returned[micro][0],
            returned[micro][1],
            n_dp,
            experts,
            capacity,
        )
        outputs.append(moe)
        grads_in.append(grad_in)
    gate_shard, up_shard, down_shard = (
        lax.psum_scatter(gate_sum, "dp", scatter_dimension=0, tiled=True),
        lax.psum_scatter(up_sum, "dp", scatter_dimension=0, tiled=True),
        lax.psum_scatter(down_sum, "dp", scatter_dimension=0, tiled=True),
    )
    return (jnp.stack(outputs), jnp.stack(grads_in), gate_shard, up_shard, down_shard)


def solution(mesh):
    return jax.shard_map(
        local,
        mesh=mesh,
        in_specs=(
            P(None, ("dp", "expert"), None),
            P(None, ("dp", "expert"), None),
            P(None, ("dp", "expert"), None),
            P(None, ("dp", "expert"), None),
            P(),
            P(None, "expert"),
            P(None, "expert"),
            P(None, "expert"),
        ),
        out_specs=(
            P(None, ("dp", "expert"), None),
            P(None, ("dp", "expert"), None),
            P("dp", "expert"),
            P("dp", "expert"),
            P("dp", "expert"),
        ),
        check_vma=False,
    )
```

profile of v0, /device:TPU:0, one launch (start us, length us, event | category | flops | bytes accessed | tf_op | source)
XLA Modules:
  0.0 558.6 jit_solution(1557309975846956298)
XLA Ops:
  7.2 0.7 slice_bitcast_fusion.7
  8.4 0.1 reduce_window_sum.17
  8.5 0.1 reduce_window_sum.18
  8.6 0.8 slice_bitcast_fusion.5
  9.3 0.2 select_reduce_fusion
  10.5 1.3 convolution_convert_fusion.4
  11.8 1.3 convolution_convert_fusion.3
  13.1 0.1 broadcast_in_dim.59
  13.3 0.1 broadcast_in_dim.61
  13.4 2.3 pad_maximum_fusion
  15.7 7.4 %all-to-all-start = ((bf16[32,16,3584]{2,1,0:T(8,128)(2,1)}), bf16[32,16,3584]{2,1,0:T(8,128)(2,1)}, u32[]{:S(2)}, u32[]{:S(2)}) async-start(bf16[32,16,3584]{2,1,0:T(8,128)(2,1)} %pad_maximum_fusion), calls=%async_computation | async-start | bytes 7340032 | tf_op jit(solution)/shard_map/all_to_all | solution.py:104
  23.3 0.4 multiply_convert_fusion.3
  23.7 0.1 convert_element_type.157
  23.8 0.1 convert_element_type.162
  24.0 0.5 convolution_convert_fusion.2
  24.5 0.5 convolution_convert_fusion.1
  25.0 0.1 broadcast_in_dim.66
  25.1 0.1 broadcast_in_dim.68
  25.3 2.3 pad_maximum_fusion.1
  27.5 79.4 %all-to-all-done = bf16[32,16,3584]{2,1,0:T(8,128)(2,1)} async-done(((bf16[32,16,3584]{2,1,0:T(8,128)(2,1)}), bf16[32,16,3584]{2,1,0:T(8,128)(2,1)}, u32[]{:S(2)}, u32[]{:S(2)}) %all-to-all-start) | async-done | bytes 3670048 | tf_op jit(solution)/shard_map/all_to_all | solution.py:104
  107.0 3.6 all-to-all-start.2
  110.6 5.3 fusion.33
  115.9 5.1 fusion.34
  121.0 73.4 %all-to-all-done.2 = bf16[32,16,3584]{2,1,0:T(8,128)(2,1)} async-done(((bf16[32,16,3584]{2,1,0:T(8,128)(2,1)}), bf16[32,16,3584]{2,1,0:T(8,128)(2,1)}, u32[]{:S(2)}, u32[]{:S(2)}) %all-to-all-start.2) | async-done | bytes 3670048 | tf_op jit(solution)/shard_map/all_to_all | solution.py:105
  194.4 5.8 %multiply_convert_fusion = (bf16[512,512]{1,0:T(8,128)(2,1)S(1)}, bf16[512,512]{1,0:T(8,128)(2,1)S(1)}, bf16[512,512]{1,0:T(8,128)(2,1)S(1)}) fusion(f32[512,512]{1,0:T(8,128)S(1)} %fusion.33, f32[512,512]{1,0:T(8,128)} %fusion.34, bf16[512,3584]{1,0:T(8,128)(2,1)} %bitcast.34, bf16[3584,512]{1,0:T(8,128)(2,1)} %param.15), kind=kOutput, calls=%fused_computation.20 | convolution fusion | flops 1882980352 | bytes 11010048 | tf_op jit(solution)/shard_map/dot_general | solution.py:88
  200.2 7.1 %fusion.38 = f32[3584,512]{1,0:T(8,128)} fusion(bf16[512,3584]{1,0:T(8,128)(2,1)} %bitcast.34, bf16[512,512]{1,0:T(8,128)(2,1)S(1)} %get-tuple-element.15), kind=kOutput, calls=%fused_computation.96 | convolution fusion | flops 1879048192 | bytes 11534336 | tf_op jit(solution)/shard_map/dot_general | solution.py:87
  207.3 0.2 reduce-scatter.4.cloned.1.call-start
  207.5 7.2 %fusion.36 = f32[3584,512]{1,0:T(8,128)} fusion(bf16[512,3584]{1,0:T(8,128)(2,1)} %bitcast.14, bf16[512,512]{1,0:T(8,128)(2,1)S(1)} %get-tuple-element.14), kind=kOutput, calls=%fused_computation.94 | convolution fusion | flops 1879048192 | bytes 11534336 | tf_op jit(solution)/shard_map/dot_general | solution.py:93
  214.7 4.3 fusion.35
  219.0 3.9 add_convert_fusion
  223.0 3.6 all-to-all-start.3
  226.6 7.1 %fusion.37 = f32[3584,512]{1,0:T(8,128)} fusion(bf16[512,3584]{1,0:T(8,128)(2,1)} %bitcast.14, bf16[512,512]{1,0:T(8,128)(2,1)S(1)} %get-tuple-element.13), kind=kOutput, calls=%fused_computation.95 | convolution fusion | flops 1879048192 | bytes 11534336 | tf_op jit(solution)/shard_map/dot_general | solution.py:94
  233.7 6.0 %convolution_convert_fusion = bf16[512,3584]{1,0:T(8,128)(2,1)} fusion(bf16[512,512]{1,0:T(8,128)(2,1)S(1)} %get-tuple-element.15, bf16[3584,512]{1,0:T(8,128)(2,1)} %param.15), kind=kOutput, calls=%fused_computation.1 | convolution fusion | flops 1880883200 | bytes 7864320 | tf_op jit(solution)/shard_map/dot_general | solution.py:84
  239.7 70.9 %all-to-all-done.3 = bf16[32,16,3584]{2,1,0:T(8,128)(2,1)} async-done(((bf16[32,16,3584]{2,1,0:T(8,128)(2,1)}), bf16[32,16,3584]{2,1,0:T(8,128)(2,1)}, u32[]{:S(2)}, u32[]{:S(2)}) %all-to-all-start.3) | async-done | bytes 3670048 | tf_op jit(solution)/shard_map/all_to_all | solution.py:112
  310.6 3.8 all-to-all-start.1
  314.8 0.2 fusion.17
  315.1 0.2 fusion.15
  315.2 3.1 convert_reduce_fusion.1
  318.4 1.0 fusion.2
  319.4 1.0 fusion.3
  320.4 77.8 %all-to-all-done.1 = bf16[32,16,3584]{2,1,0:T(8,128)(2,1)} async-done(((bf16[32,16,3584]{2,1,0:T(8,128)(2,1)}), bf16[32,16,3584]{2,1,0:T(8,128)(2,1)}, u32[]{:S(2)}, u32[]{:S(2)}) %all-to-all-start.1) | async-done | bytes 3670048 | tf_op jit(solution)/shard_map/all_to_all | solution.py:111
  398.1 3.1 convert_reduce_fusion.3
  401.3 1.0 fusion
  402.3 1.0 fusion.1
  403.3 0.7 pad_maximum_fusion.3
  404.0 0.7 pad_maximum_fusion.2
  404.7 59.4 %reduce-scatter.4.cloned.1.call-done = f32[1792,512]{1,0:T(8,128)} async-done(((f32[3584,512]{1,0:T(8,128)}), f32[1792,512]{1,0:T(8,128)}) %reduce-scatter.4.cloned.1.call-update) | async-done | bytes 3670032 | tf_op jit(solution)/shard_map/reduce_scatter | solution.py:171
  464.1 88.0 %reduce-scatter.6.cloned.1.call-done = f32[1792,512]{1,0:T(8,128)} async-done(((f32[3584,512]{1,0:T(8,128)}), f32[1792,512]{1,0:T(8,128)}) %reduce-scatter.6.cloned.1.call-update) | async-done | bytes 3670032 | tf_op jit(solution)/shard_map/reduce_scatter | solution.py:172
  (46 shorter events, 2.2 us)
Async XLA Ops:
  15.7 7.4 %copy-start.3 = (f32[2,16,4]{1,2,0:T(4,128)S(1)}, f32[2,16,4]{1,2,0:T(4,128)}, u32[]{:S(2)}) copy-start(f32[2,16,4]{1,2,0:T(4,128)} %param.11) | copy-start | bytes 1540
  15.7 7.6 %copy-start.2 = (bf16[2,16,3584]{2,1,0:T(8,128)(2,1)S(1)}, bf16[2,16,3584]{2,1,0:T(8,128)(2,1)}, u32[]{:S(2)}) copy-start(bf16[2,16,3584]{2,1,0:T(8,128)(2,1)} %param.9) | copy-start | bytes 688132
  15.7 91.3 %all-to-all-start = ((bf16[32,16,3584]{2,1,0:T(8,128)(2,1)}), bf16[32,16,3584]{2,1,0:T(8,128)(2,1)}, u32[]{:S(2)}, u32[]{:S(2)}) async-start(bf16[32,16,3584]{2,1,0:T(8,128)(2,1)} %pad_maximum_fusion), calls=%async_computation | async-start | bytes 7340032 | tf_op jit(solution)/shard_map/all_to_all | solution.py:104
  107.0 87.4 %all-to-all-start.2 = ((bf16[32,16,3584]{2,1,0:T(8,128)(2,1)}), bf16[32,16,3584]{2,1,0:T(8,128)(2,1)}, u32[]{:S(2)}, u32[]{:S(2)}) async-start(bf16[32,16,3584]{2,1,0:T(8,128)(2,1)} %pad_maximum_fusion.1), calls=%async_computation.2 | async-start | bytes 7340032 | tf_op jit(solution)/shard_map/all_to_all | solution.py:105
  110.5 294.2 %reduce-scatter.8.cloned.1.call-start = ((), (), s32[]{:S(2)}) async-start(), calls=%async_computation.9 | async-start | bytes 11010048 | tf_op jit(solution)/shard_map/reduce_scatter | solution.py:173
  110.6 5.4 copy-start
  207.3 256.8 %reduce-scatter.4.cloned.1.call-start = ((), (), s32[]{:S(2)}) async-start(), calls=%async_computation.7 | async-start | bytes 11010048 | tf_op jit(solution)/shard_map/reduce_scatter | solution.py:171
  214.7 4.3 copy-start.1
  223.0 87.6 %all-to-all-start.3 = ((bf16[32,16,3584]{2,1,0:T(8,128)(2,1)}), bf16[32,16,3584]{2,1,0:T(8,128)(2,1)}, u32[]{:S(2)}, u32[]{:S(2)}) async-start(bf16[32,16,3584]{2,1,0:T(8,128)(2,1)} %bitcast.104), calls=%async_computation.3 | async-start | bytes 7340032 | tf_op jit(solution)/shard_map/all_to_all | solution.py:112
  226.6 325.5 %reduce-scatter.6.cloned.1.call-start = ((), (), s32[]{:S(2)}) async-start(), calls=%async_computation.8 | async-start | bytes 11010048 | tf_op jit(solution)/shard_map/reduce_scatter | solution.py:172
  310.6 87.6 %all-to-all-start.1 = ((bf16[32,16,3584]{2,1,0:T(8,128)(2,1)}), bf16[32,16,3584]{2,1,0:T(8,128)(2,1)}, u32[]{:S(2)}, u32[]{:S(2)}) async-start(bf16[32,16,3584]{2,1,0:T(8,128)(2,1)} %bitcast.113), calls=%async_computation.1 | async-start | bytes 7340032 | tf_op jit(solution)/shard_map/all_to_all | solution.py:111
Sparse Core Ops, SparseCore 0:
  207.4 154.0 reduce-scatter.7
  364.5 99.5 reduce-scatter.3
  467.0 85.0 reduce-scatter.5
where the time goes:
time: 559 us
  waiting for transfers between devices  449 us (80%)
  matrix products  59.7 us (11%)
  starting transfers between devices  18.6 us (3%)
  between operations  14.1 us (3%)
  other arithmetic  13.7 us (2%)
    reduce_scatter x1, waiting for transfers between devices, local(): lax.psum_scatter(up_sum, 'dp', scatter_dimension=0, tiled=True)  88 us
    all_to_all x1, waiting for transfers between devices, send_out(): lax.all_to_all(moved, ('dp', 'expert'), split_axis=0, concat_axis=0, tile...  79.4 us
    all_to_all x1, waiting for transfers between devices, send_back(): lax.all_to_all(part_out, ('dp', 'expert'), split_axis=0, concat_axis=0, t...  77.8 us
    all_to_all x1, waiting for transfers between devices, send_out(): lax.all_to_all(spread, ('dp', 'expert'), split_axis=0, concat_axis=0, til...  73.4 us
    all_to_all x1, waiting for transfers between devices, send_back(): lax.all_to_all(part_dx, ('dp', 'expert'), split_axis=0, concat_axis=0, ti...  70.9 us
    reduce_scatter x1, waiting for transfers between devices, local(): lax.psum_scatter(gate_sum, 'dp', scatter_dimension=0, tiled=True)  59.4 us
  transfers between devices with their start and end apart: 7, of which 6 were waited for; matrix products, arithmetic and copies ran while one was open for 10% of the time, Pallas kernels for 0%

commit v1 on v0

v1 whole, which is shorter than its diff:
```python
import functools

import jax
import jax.numpy as jnp
from jax import lax
from jax.experimental import pallas as pl
from jax.experimental.pallas import tpu as pltpu
from jax.sharding import PartitionSpec as P

SPLIT = 2
CORES = 2
SIDES = 2
MESH = pl.DeviceIdType.MESH


def place(n_ep):
    me = lax.axis_index("expert")
    half = lax.axis_index("dp")
    core = lax.rem(me, CORES)
    side = lax.rem(lax.div(me, CORES), SIDES)
    layer = lax.div(me, CORES * SIDES)
    return half, layer, side, core


def block_of(layer, side, core):
    return (layer * SIDES + side) * CORES + core


def greet(layers, half, layer, side, core):
    barrier = pltpu.get_barrier_semaphore()
    peers = [(half, block_of(lax.rem(layer + k, layers), side, core)) for k in range(1, layers)]
    peers.append((half, block_of(layer, 1 - side, core)))
    peers.append((half, block_of(layer, side, 1 - core)))
    peers.append((1 - half, block_of(layer, side, core)))
    for peer in peers:
        pl.semaphore_signal(barrier, inc=1, device_id=peer, device_id_type=MESH)
    pl.semaphore_wait(barrier, len(peers))


def remote(src, dst, send, recv, peer):
    return pltpu.make_async_remote_copy(
        src_ref=src, dst_ref=dst, send_sem=send, recv_sem=recv, device_id=peer, device_id_type=MESH
    )


def gather_kernel(
    layers, t_ref, g_ref, w_ref, own_t, own_g, own_w, oth_t, oth_g,
    local_sem, zs, zr, xs, xr, cs, cr, ys, yr, fs, fr,
):
    half, layer, side, core = place(layers)
    me = block_of(layer, side, core)
    width = oth_t.shape[2]
    greet(layers, half, layer, side, core)
    own_in = (t_ref, g_ref, w_ref)
    own = (own_t, own_g, own_w)
    oth = (oth_t, oth_g)
    across = (half, block_of(layer, 1 - side, core))
    sibling = (half, block_of(layer, side, 1 - core))
    partner = (1 - half, me)
    cols = pl.ds(pl.multiple_of((1 - half) * width, 128), width)
    started = []

    def go(copy):
        copy.start()
        started.append(copy)
        return copy

    locals_ = []
    for a in range(3):
        copy = pltpu.make_async_copy(own_in[a], own[a].at[me], local_sem.at[a])
        copy.start()
        locals_.append(copy)
    z_in = {}
    for a in (2, 0, 1):
        for k in range(1, layers):
            peer = (half, block_of(lax.rem(layer + k, layers), side, core))
            z_in[a, k] = go(remote(own_in[a], own[a].at[me], zs.at[a, k], zr.at[a, k], peer))

    def hand_on(a, src, b, k, slot_x):
        if slot_x is not None:
            go(remote(src, own[a].at[b], xs.at[a, slot_x], xr.at[a, slot_x], across))
        if a < 2:
            part = src.at[:, cols]
            go(remote(part, oth[a].at[b], ys.at[a, k], yr.at[a, k], partner))
        go(remote(src, own[a].at[b], cs.at[a, k], cr.at[a, k], sibling))

    def from_side(k):
        b = block_of(lax.rem(layer - k + layers, layers), 1 - side, core)
        for a in (2, 0, 1):
            remote(own[a].at[b], own[a].at[b], xs.at[a, k], xr.at[a, k], across).wait_recv()
            hand_on(a, own[a].at[b], b, layers + k, None)

    for k in range(layers):
        b = block_of(lax.rem(layer - k + layers, layers), side, core)
        for a in (2, 0, 1):
            if k > 0:
                z_in[a, k].wait_recv()
            src = own_in[a] if k == 0 else own[a].at[b]
            hand_on(a, src, b, k, k)
        if k > 0:
            from_side(k - 1)
    from_side(layers - 1)

    def source(k, c):
        s = side if k < layers else 1 - side
        return block_of(lax.rem(layer - k % layers + layers, layers), s, c)

    for k in range(2 * layers):
        b = source(k, core)
        for a in range(2):
            dst = oth[a].at[b]
            remote(dst, dst, ys.at[a, k], yr.at[a, k], partner).wait_recv()
            go(remote(dst, dst, fs.at[a, k], fr.at[a, k], sibling))
    for k in range(2 * layers):
        b = source(k, 1 - core)
        for a in range(3):
            dst = own[a].at[b]
            remote(dst, dst, cs.at[a, k], cr.at[a, k], sibling).wait_recv()
        for a in range(2):
            dst = oth[a].at[b]
            remote(dst, dst, fs.at[a, k], fr.at[a, k], sibling).wait_recv()
    for copy in locals_:
        copy.wait()
    for copy in started:
        copy.wait_send()


def gather(layers, tokens, cots, weights):
    rows, width = tokens.shape
    blocks = layers * SIDES * CORES
    dma = pltpu.SemaphoreType.DMA
    anywhere = pl.BlockSpec(memory_space=pl.ANY)
    moved = blocks * rows * width * 6
    return pl.pallas_call(
        functools.partial(gather_kernel, layers),
        out_shape=(
            jax.ShapeDtypeStruct((blocks, rows, width), tokens.dtype),
            jax.ShapeDtypeStruct((blocks, rows, width), cots.dtype),
            jax.ShapeDtypeStruct((blocks, rows, weights.shape[1]), weights.dtype),
            jax.ShapeDtypeStruct((blocks, rows, width // 2), tokens.dtype),
            jax.ShapeDtypeStruct((blocks, rows, width // 2), cots.dtype),
        ),
        in_specs=[anywhere] * 3,
        out_specs=(anywhere,) * 5,
        scratch_shapes=[
            dma((3,)),
            dma((3, layers)), dma((3, layers)),
            dma((3, layers)), dma((3, layers)),
            dma((3, 2 * layers)), dma((3, 2 * layers)),
            dma((2, 2 * layers)), dma((2, 2 * layers)),
            dma((2, 2 * layers)), dma((2, 2 * layers)),
        ],
        compiler_params=pltpu.CompilerParams(collective_id=0, has_side_effects=True),
        cost_estimate=pl.CostEstimate(flops=0, bytes_accessed=moved, transcendentals=0),
        name="gather_rows",
    )(tokens, cots, weights)


def return_kernel(
    layers, r0, r1, acts, out0, out1, oth_acts, mine, from_core, from_side, from_layer,
    local_sem, cs, cr, xs, xr, zs, zr, hs, hr,
):
    half, layer, side, core = place(layers)
    greet(layers, half, layer, side, core)
    width = out0.shape[1]
    step = next(s for s in (512, 256, 128) if width % s == 0)
    across = (half, block_of(layer, 1 - side, core))
    sibling = (half, block_of(layer, side, 1 - core))
    partner = (1 - half, block_of(layer, side, core))
    parts = (r0, r1)
    outs = (out0, out1)
    swap = remote(acts, oth_acts, hs, hr, partner)
    swap.start()
    core_in = {}
    local_in = {}
    for k in range(layers):
        goal = lax.rem(layer + 1 + k, layers)
        for j in range(2):
            s = 1 - side if j == 0 else side
            i = 2 * k + j
            for a in range(2):
                core_in[a, i] = remote(
                    parts[a].at[block_of(goal, s, 1 - core)], from_core.at[a, i], cs.at[a, i], cr.at[a, i], sibling
                )
                core_in[a, i].start()
                local_in[a, i] = pltpu.make_async_copy(
                    parts[a].at[block_of(goal, s, core)], mine.at[a, i], local_sem.at[a, i]
                )
                local_in[a, i].start()
    side_in = {}
    layer_in = {}

    def chunks(body):
        @pl.loop(0, width // step)
        def _(q):
            body(pl.ds(pl.multiple_of(q * step, step), step))

    f32 = jnp.float32

    def first(k):
        i = 2 * k
        for a in range(2):
            local_in[a, i].wait()
            core_in[a, i].wait_recv()

            def body(c):
                total = mine[a, i, :, c].astype(f32) + from_core[a, i, :, c].astype(f32)
                mine[a, i, :, c] = total.astype(mine.dtype)

            chunks(body)
            side_in[a, k] = remote(mine.at[a, i], from_side.at[a, k], xs.at[a, k], xr.at[a, k], across)
            side_in[a, k].start()

    def second(k):
        i = 2 * k + 1
        for a in range(2):
            local_in[a, i].wait()
            core_in[a, i].wait_recv()
            side_in[a, k].wait_recv()
            if k < layers - 1:

                def body(c):
                    total = mine[a, i, :, c].astype(f32) + from_core[a, i, :, c].astype(f32)
                    total = total + from_side[a, k, :, c].astype(f32)
                    mine[a, i, :, c] = total.astype(mine.dtype)

                chunks(body)
                goal = lax.rem(layer + 1 + k, layers)
                layer_in[a, k] = remote(
                    mine.at[a, i], from_layer.at[a, k], zs.at[a, k], zr.at[a, k], (half, block_of(goal, side, core))
                )
                layer_in[a, k].start()

    first(0)
    for k in range(layers):
        if k + 1 < layers:
            first(k + 1)
        second(k)
    for a in range(2):
        for k in range(layers - 1):
            layer_in[a, k].wait_recv()
        i = 2 * layers - 1

        def body(c):
            total = mine[a, i, :, c].astype(f32) + from_core[a, i, :, c].astype(f32)
            total = total + from_side[a, layers - 1, :, c].astype(f32)
            for k in range(layers - 1):
                total = total + from_layer[a, k, :, c].astype(f32)
            outs[a][:, c] = total.astype(outs[a].dtype)

        chunks(body)
    swap.wait()
    for copies in (core_in, side_in, layer_in):
        for copy in copies.values():
            copy.wait_send()


def give_back(layers, part_out, part_dx, acts):
    blocks, rows, width = part_out.shape
    dma = pltpu.SemaphoreType.DMA
    anywhere = pl.BlockSpec(memory_space=pl.ANY)
    whole = pl.BlockSpec(memory_space=pltpu.VMEM)
    kind = part_out.dtype
    need = rows * width * 2 * 2 * (2 * 2 * layers + layers + layers + 2)
    return pl.pallas_call(
        functools.partial(return_kernel, layers),
        out_shape=(
            jax.ShapeDtypeStruct((rows, width), kind),
            jax.ShapeDtypeStruct((rows, width), kind),
            jax.ShapeDtypeStruct(acts.shape, acts.dtype),
        ),
        in_specs=[anywhere] * 3,
        out_specs=(whole, whole, anywhere),
        scratch_shapes=[
            pltpu.VMEM((2, 2 * layers, rows, width), kind),
            pltpu.VMEM((2, 2 * layers, rows, width), kind),
            pltpu.VMEM((2, layers, rows, width), kind),
            pltpu.VMEM((2, layers - 1, rows, width), kind),
            dma((2, 2 * layers)),
            dma((2, 2 * layers)), dma((2, 2 * layers)),
            dma((2, layers)), dma((2, layers)),
            dma((2, layers - 1)), dma((2, layers - 1)),
            dma, dma,
        ],
        compiler_params=pltpu.CompilerParams(
            collective_id=1, has_side_effects=True, vmem_limit_bytes=min(need + (4 << 20), 60 << 20)
        ),
        cost_estimate=pl.CostEstimate(flops=0, bytes_accessed=need, transcendentals=0),
        name="return_rows",
    )(part_out, part_dx, acts)


def dense_weights(expert_ids, probs, marks, experts, capacity):
    tok_rows = expert_ids.shape[1]
    labels = jnp.arange(experts, dtype=jnp.int32)
    onehot = expert_ids[:, :, :, None] == labels
    chosen = jnp.any(onehot, axis=2)
    weight = jnp.sum(jnp.where(onehot, probs[:, :, :, None], 0.0), axis=2)
    at = jnp.arange(tok_rows, dtype=jnp.int32)
    before = at[None, :, None, None] > at[None, None, :, None]
    ranked = jnp.sum((before & chosen[:, None, :, :]).astype(jnp.int32), axis=2)
    limit = jnp.where(marks[:, None, :] > 0, 2 * capacity, capacity)
    return jnp.where(chosen & (ranked < limit), weight, 0.0)


def local(tokens, out_grad, expert_ids, route_probs, copy_marks, w_gate, w_up, w_down):
    n_ep = lax.axis_size("expert")
    experts = n_ep // SPLIT
    layers = n_ep // (SIDES * CORES)
    tok_rows, topk = (expert_ids.shape[1], expert_ids.shape[2])
    width = tokens.shape[2]
    rows = 2 * tok_rows
    capacity = max(1, tok_rows * topk // experts)
    half = lax.axis_index("dp")
    expert = lax.axis_index("expert") // SPLIT
    f32 = jnp.float32
    bf16 = jnp.bfloat16
    weights = dense_weights(expert_ids, route_probs, copy_marks, experts, capacity).reshape(rows, experts)
    lanes = -(-experts // 128) * 128
    weights = jnp.pad(weights, ((0, 0), (0, lanes - experts)))
    own_t, own_g, own_w, oth_t, oth_g = gather(
        layers, tokens.reshape(rows, width), out_grad.reshape(rows, width), weights
    )
    own_t = own_t.reshape(-1, width)
    own_g = own_g.reshape(-1, width)
    oth_t = oth_t.reshape(-1, width // 2)
    oth_g = oth_g.reshape(-1, width // 2)
    mine = jnp.arange(lanes, dtype=jnp.int32) == expert
    p = jnp.sum(jnp.where(mine, own_w.reshape(-1, lanes), 0.0), axis=1, keepdims=True)
    contract = (((1,), (1,)), ((), ()))
    rows_first = (((0,), (0,)), ((), ()))
    gate_pre = jnp.dot(own_t, w_gate, preferred_element_type=f32)
    up_pre = jnp.dot(own_t, w_up, preferred_element_type=f32)
    squash = jax.nn.sigmoid(gate_pre)
    active = gate_pre * squash
    hidden = (p * (active * up_pre)).astype(bf16)
    hidden_grad = p * jnp.dot(own_g, w_down, preferred_element_type=f32)
    gate_grad = (hidden_grad * up_pre * squash * (1.0 + gate_pre * (1.0 - squash))).astype(bf16)
    up_grad = (hidden_grad * active).astype(bf16)
    part_out = lax.dot_general(hidden, w_down, contract, preferred_element_type=f32).astype(bf16)
    part_dx = lax.dot_general(gate_grad, w_gate, contract, preferred_element_type=f32)
    part_dx = (part_dx + lax.dot_general(up_grad, w_up, contract, preferred_element_type=f32)).astype(bf16)
    acts = jnp.stack([gate_grad, up_grad, hidden])
    moe, grad_in, oth_acts = give_back(
        layers, part_out.reshape(-1, rows, width), part_dx.reshape(-1, rows, width), acts
    )
    my_t = lax.dynamic_slice_in_dim(own_t, half * (width // 2), width // 2, 1)
    my_g = lax.dynamic_slice_in_dim(own_g, half * (width // 2), width // 2, 1)

    def outer(near, near_act, far, far_act):
        total = lax.dot_general(near, near_act, rows_first, preferred_element_type=f32)
        return total + lax.dot_general(far, far_act, rows_first, preferred_element_type=f32)

    return (
        moe.reshape(tokens.shape),
        grad_in.reshape(tokens.shape),
        outer(my_t, gate_grad, oth_t, oth_acts[0]),
        outer(my_t, up_grad, oth_t, oth_acts[1]),
        outer(my_g, hidden, oth_g, oth_acts[2]),
    )


def solution(mesh):
    return jax.shard_map(
        local,
        mesh=mesh,
        in_specs=(
            P(None, ("dp", "expert"), None),
            P(None, ("dp", "expert"), None),
            P(None, ("dp", "expert"), None),
            P(None, ("dp", "expert"), None),
            P(),
            P(None, "expert"),
            P(None, "expert"),
            P(None, "expert"),
        ),
        out_specs=(
            P(None, ("dp", "expert"), None),
            P(None, ("dp", "expert"), None),
            P("dp", "expert"),
            P("dp", "expert"),
            P("dp", "expert"),
        ),
        check_vma=False,
    )
```

time: 559 us -> 173 us (0.31)
  waiting for transfers between devices: 449 us -> 0 us
  Pallas kernels: 0 us -> 134 us
  matrix products: 59.7 us -> 30.5 us
  starting transfers between devices: 18.6 us -> 0 us
  between operations: 14.1 us -> 0.83 us
  other arithmetic: 13.7 us -> 4.07 us
    all_to_all x4 -> x0, waiting for transfers between devices: 301 us -> none  [the longest x1 79.4 us: send_out(): lax.all_to_all(moved, ('dp', 'expert'), split_axis=0, concat_axis=0, tile...]
    reduce_scatter x3 -> x0, waiting for transfers between devices: 147 us -> none  [the longest x1 88 us: local(): lax.psum_scatter(up_sum, 'dp', scatter_dimension=0, tiled=True)]
    pallas_call x0 -> x2, Pallas kernels: none -> 134 us  [the longest x1 69 us: gather(): pl.pallas_call(functools.partial(gather_kernel, layers), out_shape=(jax.S...]
    dot_general x19 -> x12, matrix products: 59.7 us -> 30.5 us  [the longest x3 9.09 us: outer(): lax.dot_general(far, far_act, rows_first, preferred_element_type=f32)]
    all_to_all x4 -> x0, starting transfers between devices: 18.3 us -> none  [the longest x1 7.42 us: send_out(): lax.all_to_all(moved, ('dp', 'expert'), split_axis=0, concat_axis=0, tile...]
  transfers between devices with their start and end apart: 7 -> 0, of which waited for: 6 -> 0; matrix products, arithmetic and copies ran while one was open for 10% -> 0% of each run, Pallas kernels for 0% -> 0%
where the time goes in v1:
time: 173 us
  Pallas kernels  134 us (77%)
  matrix products  30.5 us (18%)
  other arithmetic  4.07 us (2%)
  local copies, waits for them, and re-layouts  3.67 us (2%)
    pallas_call x1, Pallas kernels, gather(): pl.pallas_call(functools.partial(gather_kernel, layers), out_shape=(jax.S...  69 us
    pallas_call x1, Pallas kernels, give_back(): pl.pallas_call(functools.partial(return_kernel, layers), out_shape=(jax.S...  64.9 us
    dot_general x3, matrix products, outer(): lax.dot_general(far, far_act, rows_first, preferred_element_type=f32)  9.09 us
    dot_general x1, matrix products, local(): gate_pre = jnp.dot(own_t, w_gate, preferred_element_type=f32)  5.34 us
    dot_general x3, matrix products, outer(): lax.dot_general(near, near_act, rows_first, preferred_element_type=f32)  5.18 us

profile of v1, /device:TPU:0, one launch (start us, length us, event | category | flops | bytes accessed | tf_op | source)
XLA Modules:
  0.0 172.9 jit_solution(13788163763779242822)
XLA Ops:
  0.7 0.7 fusion.13
  1.4 0.6 convert_reduce_fusion
  2.0 0.1 copy.15
  2.1 0.7 select_reduce_fusion.1
  2.8 0.7 compare_select_fusion
  3.5 0.1 and_select_fusion
  3.5 0.1 copy.16
  3.6 0.6 pad.4.w_ref
  4.2 69.0 %gather_rows.1 = (bf16[16,32,3584]{2,1,0:T(8,128)(2,1)}, bf16[16,32,3584]{2,1,0:T(8,128)(2,1)}, f32[16,32,128]{2,1,0:T(8,128)}, bf16[16,32,1792]{2,1,0:T(8,128)(2,1)}, bf16[16,32,1792]{2,1,0:T(8,128)(2,1)}) custom-call(bf16[32,3584]{1,0:T(8,128)(2,1)} %bitcast.51, bf16[32,3584]{1,0:T(8,128)(2,1)} %bitcast.52, f32[32,128]{1,0:T(8,128)} %pad.4.w_ref), custom_call_target="tpu_custom_call" | custom-call | bytes 11010048 | tf_op jit(solution)/shard_map/gather_rows/pallas_call | solution.py:134
  73.2 1.1 select_reduce_fusion
  74.3 0.1 mul.41
  74.4 0.0 copy-start.2
  74.4 0.0 copy-start.6
  74.4 5.3 %fusion.17 = f32[512,512]{1,0:T(8,128)S(1)} fusion(bf16[512,3584]{1,0:T(8,128)(2,1)} %bitcast.54, bf16[3584,512]{1,0:T(8,128)(2,1)} %param.13), kind=kOutput, calls=%fused_computation.36 | convolution fusion | flops 1879048192 | bytes 8388608 | tf_op jit(solution)/shard_map/dot_general | solution.py:332
  79.7 0.0 copy-done.2
  79.7 0.0 copy-done.6
  79.8 0.0 copy-start.5
  79.8 0.0 copy-start.8
  79.8 2.1 %fusion.18 = f32[512,512]{1,0:T(8,128)S(1)} fusion(bf16[512,3584]{1,0:T(8,128)(2,1)S(1)} %bitcast.55, bf16[3584,512]{1,0:T(8,128)(2,1)S(1)} %copy-done.2), kind=kOutput, calls=%fused_computation.37 | convolution fusion | flops 1879048192 | bytes 8388608 | tf_op jit(solution)/shard_map/dot_general | solution.py:333
  81.8 0.0 copy-done.5
  81.8 1.1 copy-done.8
  82.9 0.0 copy-start.3
  82.9 2.5 %multiply_convert_fusion = (bf16[512,512]{1,0:T(8,128)(2,1)S(1)}, bf16[512,512]{1,0:T(8,128)(2,1)S(1)}, bf16[512,512]{1,0:T(8,128)(2,1)S(1)}) fusion(f32[512,512]{1,0:T(8,128)S(1)} %fusion.17, f32[512,512]{1,0:T(8,128)S(1)} %fusion.18, f32[512]{0:T(512)S(1)} %mul.41, bf16[512,3584]{1,0:T(8,128)(2,1)S(1)} %bitcast.59, bf16[3584,512]{1,0:T(8,128)(2,1)S(1)} %copy-done.5), kind=kOutput, calls=%fused_computation.13 | convolution fusion | flops 1883504640 | bytes 11012096 | tf_op jit(solution)/shard_map/dot_general | solution.py:337
  85.4 0.0 copy-start.4
  85.4 0.2 pad_maximum_fusion.acts
  85.6 0.0 copy-done.3
  85.6 2.1 %fusion.19 = f32[512,3584]{1,0:T(8,128)S(1)} fusion(bf16[512,512]{1,0:T(8,128)(2,1)S(1)} %get-tuple-element.22, bf16[3584,512]{1,0:T(8,128)(2,1)S(1)} %copy-done.3), kind=kOutput, calls=%fused_computation.38 | convolution fusion | flops 1879048192 | bytes 11534336 | tf_op jit(solution)/shard_map/dot_general | solution.py:341
  87.7 2.1 %add_convert_fusion = bf16[512,3584]{1,0:T(8,128)(2,1)S(1)} fusion(f32[512,3584]{1,0:T(8,128)S(1)} %fusion.19, bf16[512,512]{1,0:T(8,128)(2,1)S(1)} %get-tuple-element.21, bf16[3584,512]{1,0:T(8,128)(2,1)S(1)} %copy-done.2), kind=kOutput, calls=%fused_computation | convolution fusion | flops 1882718208 | bytes 15204352 | tf_op jit(solution)/shard_map/dot_general | solution.py:342
  89.8 0.0 copy-done.4
  89.8 2.1 %convolution_convert_fusion = bf16[512,3584]{1,0:T(8,128)(2,1)S(1)} fusion(bf16[512,512]{1,0:T(8,128)(2,1)S(1)} %get-tuple-element.23, bf16[3584,512]{1,0:T(8,128)(2,1)S(1)} %copy-done.5), kind=kOutput, calls=%fused_computation.1 | convolution fusion | flops 1880883200 | bytes 7864320 | tf_op jit(solution)/shard_map/dot_general | solution.py:340
  92.0 64.9 %return_rows.1 = (bf16[32,3584]{1,0:T(8,128)(2,1)S(1)}, bf16[32,3584]{1,0:T(8,128)(2,1)S(1)}, bf16[3,512,512]{2,1,0:T(8,128)(2,1)S(1)}) custom-call(bf16[16,32,3584]{2,1,0:T(8,128)(2,1)S(1)} %bitcast.42, bf16[16,32,3584]{2,1,0:T(8,128)(2,1)S(1)} %bitcast.41, bf16[3,512,512]{2,1,0:T(8,128)(2,1)S(1)} %pad_maximum_fusion.acts), custom_call_target="tpu_custom_call" | custom-call | bytes 11927552 | tf_op jit(solution)/shard_map/return_rows/pallas_call | solution.py:265
  156.9 0.0 copy-start.1
  156.9 2.9 %fusion = f32[1792,512]{1,0:T(8,128)S(1)} fusion(bf16[512,512]{1,0:T(8,128)(2,1)} %copy-done.4, bf16[512,3584]{1,0:T(8,128)(2,1)} %bitcast.58, s32[]{:T(128)S(6)} %select_n.37), kind=kOutput, calls=%fused_computation.5 | convolution fusion | flops 939524096 | bytes 6029316 | tf_op jit(solution)/shard_map/dot_general | solution.py:351
  159.8 0.0 copy-done.1
  159.8 0.0 copy-start.7
  159.8 3.0 %convolution_add_fusion = f32[1792,512]{1,0:T(8,128)} fusion(f32[1792,512]{1,0:T(8,128)S(1)} %fusion, bf16[512,1792]{1,0:T(8,128)(2,1)S(1)} %bitcast.47, bf16[3,512,512]{2,1,0:T(8,128)(2,1)S(1)} %get-tuple-element.19), kind=kOutput, calls=%fused_computation.2 | convolution fusion | flops 940441600 | bytes 9699328 | tf_op jit(solution)/shard_map/dot_general | solution.py:352
  162.8 0.0 copy-done.7
  162.8 0.0 copy-start
  162.8 1.2 fusion.2
  164.0 0.3 copy-done
  164.3 3.0 %convolution_add_fusion.1 = f32[1792,512]{1,0:T(8,128)} fusion(f32[1792,512]{1,0:T(8,128)S(1)} %fusion.2, bf16[512,1792]{1,0:T(8,128)(2,1)S(1)} %bitcast.45, bf16[3,512,512]{2,1,0:T(8,128)(2,1)S(1)} %get-tuple-element.19), kind=kOutput, calls=%fused_computation.3 | convolution fusion | flops 940441600 | bytes 9699328 | tf_op jit(solution)/shard_map/dot_general | solution.py:352
  167.4 1.2 fusion.4
  168.5 3.0 %convolution_add_fusion.2 = f32[1792,512]{1,0:T(8,128)} fusion(f32[1792,512]{1,0:T(8,128)S(1)} %fusion.4, bf16[512,1792]{1,0:T(8,128)(2,1)S(1)} %bitcast.46, bf16[3,512,512]{2,1,0:T(8,128)(2,1)S(1)} %get-tuple-element.19), kind=kOutput, calls=%fused_computation.4 | convolution fusion | flops 940441600 | bytes 9699328 | tf_op jit(solution)/shard_map/dot_general | solution.py:352
  171.5 0.7 copy.19
  172.2 0.7 copy.20
  (2 shorter events, 0.0 us)
Async XLA Ops:
  74.4 5.4 %copy-start.2 = (bf16[3584,512]{1,0:T(8,128)(2,1)S(1)}, bf16[3584,512]{1,0:T(8,128)(2,1)}, u32[]{:S(2)}) copy-start(bf16[3584,512]{1,0:T(8,128)(2,1)} %param.14) | copy-start | bytes 11010052
  74.4 5.4 %copy-start.6 = (bf16[16,32,3584]{2,1,0:T(8,128)(2,1)S(1)}, bf16[16,32,3584]{2,1,0:T(8,128)(2,1)}, u32[]{:S(2)}) copy-start(bf16[16,32,3584]{2,1,0:T(8,128)(2,1)} %get-tuple-element.14) | copy-start | bytes 11010052
  79.8 2.1 %copy-start.5 = (bf16[3584,512]{1,0:T(8,128)(2,1)S(1)}, bf16[3584,512]{1,0:T(8,128)(2,1)}, u32[]{:S(2)}) copy-start(bf16[3584,512]{1,0:T(8,128)(2,1)} %param.15) | copy-start | bytes 11010052
  79.8 3.2 %copy-start.8 = (bf16[16,32,3584]{2,1,0:T(8,128)(2,1)S(1)}, bf16[16,32,3584]{2,1,0:T(8,128)(2,1)}, u32[]{:S(2)}) copy-start(bf16[16,32,3584]{2,1,0:T(8,128)(2,1)} %get-tuple-element.15) | copy-start | bytes 11010052
  82.9 2.7 %copy-start.3 = (bf16[3584,512]{1,0:T(8,128)(2,1)S(1)}, bf16[3584,512]{1,0:T(8,128)(2,1)}, u32[]{:S(2)}) copy-start(bf16[3584,512]{1,0:T(8,128)(2,1)} %param.13) | copy-start | bytes 11010052
  85.4 4.4 %copy-start.4 = (bf16[512,512]{1,0:T(8,128)(2,1)}, bf16[512,512]{1,0:T(8,128)(2,1)S(1)}, u32[]{:S(2)}) copy-start(bf16[512,512]{1,0:T(8,128)(2,1)S(1)} %get-tuple-element.23) | copy-start | bytes 1572868
  156.9 2.9 %copy-start.1 = (bf16[16,32,1792]{2,1,0:T(8,128)(2,1)S(1)}, bf16[16,32,1792]{2,1,0:T(8,128)(2,1)}, u32[]{:S(2)}) copy-start(bf16[16,32,1792]{2,1,0:T(8,128)(2,1)} %get-tuple-element.20) | copy-start | bytes 5505028
  159.8 3.0 %copy-start.7 = (bf16[16,32,3584]{2,1,0:T(8,128)(2,1)S(1)}, bf16[16,32,3584]{2,1,0:T(8,128)(2,1)}, u32[]{:S(2)}) copy-start(bf16[16,32,3584]{2,1,0:T(8,128)(2,1)} %get-tuple-element.14) | copy-start | bytes 11010052
  162.8 1.5 copy-start

commit v2 on v1

--- a/solution.py
+++ b/solution.py
@@ -58,71 +58,138 @@
     sibling = (half, block_of(layer, side, 1 - core))
     partner = (1 - half, me)
     cols = pl.ds(pl.multiple_of((1 - half) * width, 128), width)
-    started = []
-
-    def go(copy):
-        copy.start()
-        started.append(copy)
-        return copy
+    slots = 2 * layers - 1
+    arrays = (2, 0, 1)
+
+    def reach(n):
+        if n == 0:
+            return True, layer
+        if n < layers:
+            return layer >= n, layer - n
+        return layer + (n - layers + 1) < layers, layer + (n - layers + 1)
+
+    def given(condition, body):
+        if condition is True:
+            body()
+        else:
+            pl.when(condition)(body)
+
+    def along_copy(a, src, b, up, step):
+        n = step if up else layers - 1 + step
+        there = layer + 1 if up else layer - 1
+        return remote(src, own[a].at[b], zs.at[a, n], zr.at[a, n], (half, block_of(there, side, core)))
+
+    def copies(a, src, b, n, through):
+        found = []
+        if not through:
+            found.append(remote(src, own[a].at[b], xs.at[a, n], xr.at[a, n], across))
+        m = n + slots if through else n
+        if a < 2:
+            found.append(remote(src.at[:, cols], oth[a].at[b], ys.at[a, m], yr.at[a, m], partner))
+        found.append(remote(src, own[a].at[b], cs.at[a, m], cr.at[a, m], sibling))
+        return found
 
     locals_ = []
     for a in range(3):
         copy = pltpu.make_async_copy(own_in[a], own[a].at[me], local_sem.at[a])
         copy.start()
         locals_.append(copy)
-    z_in = {}
-    for a in (2, 0, 1):
-        for k in range(1, layers):
-            peer = (half, block_of(lax.rem(layer + k, layers), side, core))
-            z_in[a, k] = go(remote(own_in[a], own[a].at[me], zs.at[a, k], zr.at[a, k], peer))
-
-    def hand_on(a, src, b, k, slot_x):
-        if slot_x is not None:
-            go(remote(src, own[a].at[b], xs.at[a, slot_x], xr.at[a, slot_x], across))
-        if a < 2:
-            part = src.at[:, cols]
-            go(remote(part, oth[a].at[b], ys.at[a, k], yr.at[a, k], partner))
-        go(remote(src, own[a].at[b], cs.at[a, k], cr.at[a, k], sibling))
-
-    def from_side(k):
-        b = block_of(lax.rem(layer - k + layers, layers), 1 - side, core)
-        for a in (2, 0, 1):
-            remote(own[a].at[b], own[a].at[b], xs.at[a, k], xr.at[a, k], across).wait_recv()
-            hand_on(a, own[a].at[b], b, layers + k, None)
-
-    for k in range(layers):
-        b = block_of(lax.rem(layer - k + layers, layers), side, core)
-        for a in (2, 0, 1):
-            if k > 0:
-                z_in[a, k].wait_recv()
-            src = own_in[a] if k == 0 else own[a].at[b]
-            hand_on(a, src, b, k, k)
-        if k > 0:
-            from_side(k - 1)
+
+    def at_start():
+        for a in arrays:
+            for up in (True, False):
+                ok = layer + 1 < layers if up else layer > 0
+                pl.when(ok)(lambda a=a, up=up: along_copy(a, own_in[a], me, up, 1).start())
+            for copy in copies(a, own_in[a], me, 0, False):
+                copy.start()
+
+    def arrived(n):
+        ok, origin = reach(n)
+        up = n < layers
+        step = n if up else n - layers + 1
+
+        def body():
+            b = block_of(origin, side, core)
+            for a in arrays:
+                dst = own[a].at[b]
+                remote(dst, dst, zs.at[a, n], zr.at[a, n], sibling).wait_recv()
+                if step + 1 < layers:
+                    more = layer + 1 < layers if up else layer > 0
+                    pl.when(more)(lambda a=a, dst=dst: along_copy(a, dst, b, up, step + 1).start())
+                for copy in copies(a, dst, b, n, False):
+                    copy.start()
+
+        given(ok, body)
+
+    def from_side(n):
+        ok, origin = reach(n)
+
+        def body():
+            b = block_of(origin, 1 - side, core)
+            for a in arrays:
+                dst = own[a].at[b]
+                remote(dst, dst, xs.at[a, n], xr.at[a, n], across).wait_recv()
+                for copy in copies(a, dst, b, n, True):
+                    copy.start()
+
+        given(ok, body)
+
+    at_start()
+    for step in range(1, layers):
+        arrived(step)
+        arrived(layers - 1 + step)
+        if step == 1:
+            from_side(0)
+        else:
+            from_side(step - 1)
+            from_side(layers + step - 2)
     from_side(layers - 1)
-
-    def source(k, c):
-        s = side if k < layers else 1 - side
-        return block_of(lax.rem(layer - k % layers + layers, layers), s, c)
-
-    for k in range(2 * layers):
-        b = source(k, core)
+    from_side(2 * layers - 2)
+
+    def each(body):
+        for through in (False, True):
+            for n in range(slots):
+                ok, origin = reach(n)
+                m = n + slots if through else n
+                s = 1 - side if through else side
+                given(ok, lambda n=n, m=m, s=s, origin=origin, through=through: body(n, m, s, origin, through))
+
+    def pass_on(n, m, s, origin, through):
+        b = block_of(origin, s, core)
         for a in range(2):
             dst = oth[a].at[b]
-            remote(dst, dst, ys.at[a, k], yr.at[a, k], partner).wait_recv()
-            go(remote(dst, dst, fs.at[a, k], fr.at[a, k], sibling))
-    for k in range(2 * layers):
-        b = source(k, 1 - core)
+            remote(dst, dst, ys.at[a, m], yr.at[a, m], partner).wait_recv()
+            remote(dst, dst, fs.at[a, m], fr.at[a, m], sibling).start()
+
+    def finish(n, m, s, origin, through):
+        b = block_of(origin, s, 1 - core)
         for a in range(3):
             dst = own[a].at[b]
-            remote(dst, dst, cs.at[a, k], cr.at[a, k], sibling).wait_recv()
-        for a in range(2):
-            dst = oth[a].at[b]
-            remote(dst, dst, fs.at[a, k], fr.at[a, k], sibling).wait_recv()
+            remote(dst, dst, cs.at[a, m], cr.at[a, m], sibling).wait_recv()
+            if a < 2:
+                dst = oth[a].at[b]
+                remote(dst, dst, fs.at[a, m], fr.at[a, m], sibling).wait_recv()
+        mine = block_of(origin, s, core)
+        for a in range(3):
+            for copy in copies(a, own[a].at[mine], mine, n, through):
+                copy.wait_send()
+            if a < 2:
+                dst = oth[a].at[mine]
+                remote(dst, dst, fs.at[a, m], fr.at[a, m], sibling).wait_send()
+            if not through:
+                step_up = n + 1 if n < layers else None
+                step_dn = 1 if n == 0 else (n - layers + 2 if n >= layers else None)
+                for up, step in ((True, step_up), (False, step_dn)):
+                    if step is not None and step < layers:
+                        more = layer + 1 < layers if up else layer > 0
+                        pl.when(more)(
+                            lambda a=a, up=up, step=step: along_copy(a, own[a].at[mine], mine, up, step).wait_send()
+                        )
+
+    each(pass_on)
+    each(finish)
     for copy in locals_:
         copy.wait()
-    for copy in started:
-        copy.wait_send()
 
 
 def gather(layers, tokens, cots, weights):
@@ -131,6 +198,7 @@
     dma = pltpu.SemaphoreType.DMA
     anywhere = pl.BlockSpec(memory_space=pl.ANY)
     moved = blocks * rows * width * 6
+    slots = 2 * layers - 1
     return pl.pallas_call(
         functools.partial(gather_kernel, layers),
         out_shape=(
@@ -144,11 +212,11 @@
         out_specs=(anywhere,) * 5,
         scratch_shapes=[
             dma((3,)),
-            dma((3, layers)), dma((3, layers)),
-            dma((3, layers)), dma((3, layers)),
-            dma((3, 2 * layers)), dma((3, 2 * layers)),
-            dma((2, 2 * layers)), dma((2, 2 * layers)),
-            dma((2, 2 * layers)), dma((2, 2 * layers)),
+            dma((3, slots)), dma((3, slots)),
+            dma((3, slots)), dma((3, slots)),
+            dma((3, 2 * slots)), dma((3, 2 * slots)),
+            dma((2, 2 * slots)), dma((2, 2 * slots)),
+            dma((2, 2 * slots)), dma((2, 2 * slots)),
         ],
         compiler_params=pltpu.CompilerParams(collective_id=0, has_side_effects=True),
         cost_estimate=pl.CostEstimate(flops=0, bytes_accessed=moved, transcendentals=0),

time: 173 us -> 150 us (0.87)
  Pallas kernels: 134 us -> 111 us
    pallas_call x1, Pallas kernels: 69 us -> 56.5 us  [gather(): pl.pallas_call(functools.partial(gather_kernel, layers), out_shape=(jax.S...]
    pallas_call x1, Pallas kernels: 64.9 us -> 54.7 us  [give_back(): pl.pallas_call(functools.partial(return_kernel, layers), out_shape=(jax.S...]
where the time goes in v2:
time: 150 us
  Pallas kernels  111 us (74%)
  matrix products  30.5 us (20%)
  other arithmetic  4.07 us (3%)
  local copies, waits for them, and re-layouts  3.67 us (2%)
    pallas_call x1, Pallas kernels, gather(): pl.pallas_call(functools.partial(gather_kernel, layers), out_shape=(jax.S...  56.5 us
    pallas_call x1, Pallas kernels, give_back(): pl.pallas_call(functools.partial(return_kernel, layers), out_shape=(jax.S...  54.7 us
    dot_general x3, matrix products, outer(): lax.dot_general(far, far_act, rows_first, preferred_element_type=f32)  9.09 us
    dot_general x1, matrix products, local(): gate_pre = jnp.dot(own_t, w_gate, preferred_element_type=f32)  5.35 us
    dot_general x3, matrix products, outer(): lax.dot_general(near, near_act, rows_first, preferred_element_type=f32)  5.18 us

profile of v2, /device:TPU:0, one launch (start us, length us, event | category | flops | bytes accessed | tf_op | source)
XLA Modules:
  0.0 150.2 jit_solution(959590861202921519)
XLA Ops:
  0.7 0.7 fusion.13
  1.4 0.6 convert_reduce_fusion
  2.0 0.1 copy.15
  2.1 0.7 select_reduce_fusion.1
  2.8 0.7 compare_select_fusion
  3.5 0.1 and_select_fusion
  3.5 0.1 copy.16
  3.6 0.6 pad.4.w_ref
  4.2 56.5 %gather_rows.1 = (bf16[16,32,3584]{2,1,0:T(8,128)(2,1)}, bf16[16,32,3584]{2,1,0:T(8,128)(2,1)}, f32[16,32,128]{2,1,0:T(8,128)}, bf16[16,32,1792]{2,1,0:T(8,128)(2,1)}, bf16[16,32,1792]{2,1,0:T(8,128)(2,1)}) custom-call(bf16[32,3584]{1,0:T(8,128)(2,1)} %bitcast.51, bf16[32,3584]{1,0:T(8,128)(2,1)} %bitcast.52, f32[32,128]{1,0:T(8,128)} %pad.4.w_ref), custom_call_target="tpu_custom_call" | custom-call | bytes 11010048 | tf_op jit(solution)/shard_map/gather_rows/pallas_call | solution.py:202
  60.7 1.1 select_reduce_fusion
  61.8 0.1 mul.41
  61.9 0.0 copy-start.2
  61.9 0.0 copy-start.6
  61.9 5.3 %fusion.17 = f32[512,512]{1,0:T(8,128)S(1)} fusion(bf16[512,3584]{1,0:T(8,128)(2,1)} %bitcast.54, bf16[3584,512]{1,0:T(8,128)(2,1)} %param.13), kind=kOutput, calls=%fused_computation.36 | convolution fusion | flops 1879048192 | bytes 8388608 | tf_op jit(solution)/shard_map/dot_general | solution.py:400
  67.3 0.0 copy-done.2
  67.3 0.0 copy-done.6
  67.3 0.0 copy-start.5
  67.3 0.0 copy-start.8
  67.3 2.1 %fusion.18 = f32[512,512]{1,0:T(8,128)S(1)} fusion(bf16[512,3584]{1,0:T(8,128)(2,1)S(1)} %bitcast.55, bf16[3584,512]{1,0:T(8,128)(2,1)S(1)} %copy-done.2), kind=kOutput, calls=%fused_computation.37 | convolution fusion | flops 1879048192 | bytes 8388608 | tf_op jit(solution)/shard_map/dot_general | solution.py:401
  69.4 0.0 copy-done.5
  69.4 1.1 copy-done.8
  70.5 0.0 copy-start.3
  70.5 2.5 %multiply_convert_fusion = (bf16[512,512]{1,0:T(8,128)(2,1)S(1)}, bf16[512,512]{1,0:T(8,128)(2,1)S(1)}, bf16[512,512]{1,0:T(8,128)(2,1)S(1)}) fusion(f32[512,512]{1,0:T(8,128)S(1)} %fusion.17, f32[512,512]{1,0:T(8,128)S(1)} %fusion.18, f32[512]{0:T(512)S(1)} %mul.41, bf16[512,3584]{1,0:T(8,128)(2,1)S(1)} %bitcast.59, bf16[3584,512]{1,0:T(8,128)(2,1)S(1)} %copy-done.5), kind=kOutput, calls=%fused_computation.13 | convolution fusion | flops 1883504640 | bytes 11012096 | tf_op jit(solution)/shard_map/dot_general | solution.py:405
  72.9 0.0 copy-start.4
  73.0 0.2 pad_maximum_fusion.acts
  73.1 0.0 copy-done.3
  73.1 2.1 %fusion.19 = f32[512,3584]{1,0:T(8,128)S(1)} fusion(bf16[512,512]{1,0:T(8,128)(2,1)S(1)} %get-tuple-element.22, bf16[3584,512]{1,0:T(8,128)(2,1)S(1)} %copy-done.3), kind=kOutput, calls=%fused_computation.38 | convolution fusion | flops 1879048192 | bytes 11534336 | tf_op jit(solution)/shard_map/dot_general | solution.py:409
  75.3 2.1 %add_convert_fusion = bf16[512,3584]{1,0:T(8,128)(2,1)S(1)} fusion(f32[512,3584]{1,0:T(8,128)S(1)} %fusion.19, bf16[512,512]{1,0:T(8,128)(2,1)S(1)} %get-tuple-element.21, bf16[3584,512]{1,0:T(8,128)(2,1)S(1)} %copy-done.2), kind=kOutput, calls=%fused_computation | convolution fusion | flops 1882718208 | bytes 15204352 | tf_op jit(solution)/shard_map/dot_general | solution.py:410
  77.4 0.0 copy-done.4
  77.4 2.1 %convolution_convert_fusion = bf16[512,3584]{1,0:T(8,128)(2,1)S(1)} fusion(bf16[512,512]{1,0:T(8,128)(2,1)S(1)} %get-tuple-element.23, bf16[3584,512]{1,0:T(8,128)(2,1)S(1)} %copy-done.5), kind=kOutput, calls=%fused_computation.1 | convolution fusion | flops 1880883200 | bytes 7864320 | tf_op jit(solution)/shard_map/dot_general | solution.py:408
  79.5 54.7 %return_rows.1 = (bf16[32,3584]{1,0:T(8,128)(2,1)S(1)}, bf16[32,3584]{1,0:T(8,128)(2,1)S(1)}, bf16[3,512,512]{2,1,0:T(8,128)(2,1)S(1)}) custom-call(bf16[16,32,3584]{2,1,0:T(8,128)(2,1)S(1)} %bitcast.42, bf16[16,32,3584]{2,1,0:T(8,128)(2,1)S(1)} %bitcast.41, bf16[3,512,512]{2,1,0:T(8,128)(2,1)S(1)} %pad_maximum_fusion.acts), custom_call_target="tpu_custom_call" | custom-call | bytes 11927552 | tf_op jit(solution)/shard_map/return_rows/pallas_call | solution.py:333
  134.2 0.0 copy-start.1
  134.2 2.9 %fusion = f32[1792,512]{1,0:T(8,128)S(1)} fusion(bf16[512,512]{1,0:T(8,128)(2,1)} %copy-done.4, bf16[512,3584]{1,0:T(8,128)(2,1)} %bitcast.58, s32[]{:T(128)S(6)} %select_n.37), kind=kOutput, calls=%fused_computation.5 | convolution fusion | flops 939524096 | bytes 6029316 | tf_op jit(solution)/shard_map/dot_general | solution.py:419
  137.0 0.0 copy-done.1
  137.1 0.0 copy-start.7
  137.1 3.0 %convolution_add_fusion = f32[1792,512]{1,0:T(8,128)} fusion(f32[1792,512]{1,0:T(8,128)S(1)} %fusion, bf16[512,1792]{1,0:T(8,128)(2,1)S(1)} %bitcast.47, bf16[3,512,512]{2,1,0:T(8,128)(2,1)S(1)} %get-tuple-element.19), kind=kOutput, calls=%fused_computation.2 | convolution fusion | flops 940441600 | bytes 9699328 | tf_op jit(solution)/shard_map/dot_general | solution.py:420
  140.1 0.0 copy-done.7
  140.1 0.0 copy-start
  140.1 1.2 fusion.2
  141.3 0.3 copy-done
  141.6 3.0 %convolution_add_fusion.1 = f32[1792,512]{1,0:T(8,128)} fusion(f32[1792,512]{1,0:T(8,128)S(1)} %fusion.2, bf16[512,1792]{1,0:T(8,128)(2,1)S(1)} %bitcast.45, bf16[3,512,512]{2,1,0:T(8,128)(2,1)S(1)} %get-tuple-element.19), kind=kOutput, calls=%fused_computation.3 | convolution fusion | flops 940441600 | bytes 9699328 | tf_op jit(solution)/shard_map/dot_general | solution.py:420
  144.6 1.2 fusion.4
  145.8 3.0 %convolution_add_fusion.2 = f32[1792,512]{1,0:T(8,128)} fusion(f32[1792,512]{1,0:T(8,128)S(1)} %fusion.4, bf16[512,1792]{1,0:T(8,128)(2,1)S(1)} %bitcast.46, bf16[3,512,512]{2,1,0:T(8,128)(2,1)S(1)} %get-tuple-element.19), kind=kOutput, calls=%fused_computation.4 | convolution fusion | flops 940441600 | bytes 9699328 | tf_op jit(solution)/shard_map/dot_general | solution.py:420
  148.8 0.7 copy.19
  149.5 0.7 copy.20
  (2 shorter events, 0.0 us)
Async XLA Ops:
  61.9 5.4 %copy-start.2 = (bf16[3584,512]{1,0:T(8,128)(2,1)S(1)}, bf16[3584,512]{1,0:T(8,128)(2,1)}, u32[]{:S(2)}) copy-start(bf16[3584,512]{1,0:T(8,128)(2,1)} %param.14) | copy-start | bytes 11010052
  61.9 5.4 %copy-start.6 = (bf16[16,32,3584]{2,1,0:T(8,128)(2,1)S(1)}, bf16[16,32,3584]{2,1,0:T(8,128)(2,1)}, u32[]{:S(2)}) copy-start(bf16[16,32,3584]{2,1,0:T(8,128)(2,1)} %get-tuple-element.14) | copy-start | bytes 11010052
  67.3 2.1 %copy-start.5 = (bf16[3584,512]{1,0:T(8,128)(2,1)S(1)}, bf16[3584,512]{1,0:T(8,128)(2,1)}, u32[]{:S(2)}) copy-start(bf16[3584,512]{1,0:T(8,128)(2,1)} %param.15) | copy-start | bytes 11010052
  67.3 3.2 %copy-start.8 = (bf16[16,32,3584]{2,1,0:T(8,128)(2,1)S(1)}, bf16[16,32,3584]{2,1,0:T(8,128)(2,1)}, u32[]{:S(2)}) copy-start(bf16[16,32,3584]{2,1,0:T(8,128)(2,1)} %get-tuple-element.15) | copy-start | bytes 11010052
  70.5 2.7 %copy-start.3 = (bf16[3584,512]{1,0:T(8,128)(2,1)S(1)}, bf16[3584,512]{1,0:T(8,128)(2,1)}, u32[]{:S(2)}) copy-start(bf16[3584,512]{1,0:T(8,128)(2,1)} %param.13) | copy-start | bytes 11010052
  72.9 4.4 %copy-start.4 = (bf16[512,512]{1,0:T(8,128)(2,1)}, bf16[512,512]{1,0:T(8,128)(2,1)S(1)}, u32[]{:S(2)}) copy-start(bf16[512,512]{1,0:T(8,128)(2,1)S(1)} %get-tuple-element.23) | copy-start | bytes 1572868
  134.2 2.9 %copy-start.1 = (bf16[16,32,1792]{2,1,0:T(8,128)(2,1)S(1)}, bf16[16,32,1792]{2,1,0:T(8,128)(2,1)}, u32[]{:S(2)}) copy-start(bf16[16,32,1792]{2,1,0:T(8,128)(2,1)} %get-tuple-element.20) | copy-start | bytes 5505028
  137.1 3.0 %copy-start.7 = (bf16[16,32,3584]{2,1,0:T(8,128)(2,1)S(1)}, bf16[16,32,3584]{2,1,0:T(8,128)(2,1)}, u32[]{:S(2)}) copy-start(bf16[16,32,3584]{2,1,0:T(8,128)(2,1)} %get-tuple-element.14) | copy-start | bytes 11010052
  140.1 1.5 copy-start

commit v3 on v2

--- a/solution.py
+++ b/solution.py
@@ -265,45 +265,50 @@
 
     f32 = jnp.float32
 
-    def first(k):
+    units = [(k, a) for k in range(layers) for a in range(2)]
+
+    def first(k, a):
         i = 2 * k
-        for a in range(2):
-            local_in[a, i].wait()
-            core_in[a, i].wait_recv()
+        local_in[a, i].wait()
+        core_in[a, i].wait_recv()
+
+        def body(c):
+            total = mine[a, i, :, c].astype(f32) + from_core[a, i, :, c].astype(f32)
+            mine[a, i, :, c] = total.astype(mine.dtype)
+
+        chunks(body)
+        side_in[a, k] = remote(mine.at[a, i], from_side.at[a, k], xs.at[a, k], xr.at[a, k], across)
+
+    def second(k, a):
+        i = 2 * k + 1
+        local_in[a, i].wait()
+        core_in[a, i].wait_recv()
+        if k < layers - 1:
 
             def body(c):
                 total = mine[a, i, :, c].astype(f32) + from_core[a, i, :, c].astype(f32)
+                total = total + from_side[a, k, :, c].astype(f32)
                 mine[a, i, :, c] = total.astype(mine.dtype)
 
             chunks(body)
-            side_in[a, k] = remote(mine.at[a, i], from_side.at[a, k], xs.at[a, k], xr.at[a, k], across)
-            side_in[a, k].start()
-
-    def second(k):
-        i = 2 * k + 1
-        for a in range(2):
-            local_in[a, i].wait()
-            core_in[a, i].wait_recv()
-            side_in[a, k].wait_recv()
-            if k < layers - 1:
-
-                def body(c):
-                    total = mine[a, i, :, c].astype(f32) + from_core[a, i, :, c].astype(f32)
-                    total = total + from_side[a, k, :, c].astype(f32)
-                    mine[a, i, :, c] = total.astype(mine.dtype)
-
-                chunks(body)
-                goal = lax.rem(layer + 1 + k, layers)
-                layer_in[a, k] = remote(
-                    mine.at[a, i], from_layer.at[a, k], zs.at[a, k], zr.at[a, k], (half, block_of(goal, side, core))
-                )
-                layer_in[a, k].start()
-
-    first(0)
-    for k in range(layers):
-        if k + 1 < layers:
-            first(k + 1)
-        second(k)
+            goal = lax.rem(layer + 1 + k, layers)
+            layer_in[a, k] = remote(
+                mine.at[a, i], from_layer.at[a, k], zs.at[a, k], zr.at[a, k], (half, block_of(goal, side, core))
+            )
+            layer_in[a, k].start()
+
+    window = 2
+    for k, a in units[:window]:
+        first(k, a)
+        side_in[a, k].start()
+    for u, (k, a) in enumerate(units):
+        later = units[u + window] if u + window < len(units) else None
+        if later is not None:
+            first(*later)
+        side_in[a, k].wait_recv()
+        if later is not None:
+            side_in[later[1], later[0]].start()
+        second(k, a)
     for a in range(2):
         for k in range(layers - 1):
             layer_in[a, k].wait_recv()

time: 150 us -> 150 us (level)
  no operation moved by 1% of the time
where the time goes in v3:
time: 150 us
  Pallas kernels  111 us (74%)
  matrix products  30.5 us (20%)
  other arithmetic  4.07 us (3%)
  local copies, waits for them, and re-layouts  3.67 us (2%)
    pallas_call x1, Pallas kernels, gather(): pl.pallas_call(functools.partial(gather_kernel, layers), out_shape=(jax.S...  56.5 us
    pallas_call x1, Pallas kernels, give_back(): pl.pallas_call(functools.partial(return_kernel, layers), out_shape=(jax.S...  54.7 us
    dot_general x3, matrix products, outer(): lax.dot_general(far, far_act, rows_first, preferred_element_type=f32)  9.09 us
    dot_general x1, matrix products, local(): gate_pre = jnp.dot(own_t, w_gate, preferred_element_type=f32)  5.35 us
    dot_general x3, matrix products, outer(): lax.dot_general(near, near_act, rows_first, preferred_element_type=f32)  5.18 us

profile of v3, /device:TPU:0, one launch (start us, length us, event | category | flops | bytes accessed | tf_op | source)
XLA Modules:
  0.0 150.2 jit_solution(16992694590041355192)
XLA Ops:
  0.7 0.7 fusion.13
  1.4 0.6 convert_reduce_fusion
  2.0 0.1 copy.15
  2.1 0.7 select_reduce_fusion.1
  2.8 0.7 compare_select_fusion
  3.5 0.1 and_select_fusion
  3.5 0.1 copy.16
  3.6 0.6 pad.4.w_ref
  4.2 56.5 %gather_rows.1 = (bf16[16,32,3584]{2,1,0:T(8,128)(2,1)}, bf16[16,32,3584]{2,1,0:T(8,128)(2,1)}, f32[16,32,128]{2,1,0:T(8,128)}, bf16[16,32,1792]{2,1,0:T(8,128)(2,1)}, bf16[16,32,1792]{2,1,0:T(8,128)(2,1)}) custom-call(bf16[32,3584]{1,0:T(8,128)(2,1)} %bitcast.51, bf16[32,3584]{1,0:T(8,128)(2,1)} %bitcast.52, f32[32,128]{1,0:T(8,128)} %pad.4.w_ref), custom_call_target="tpu_custom_call" | custom-call | bytes 11010048 | tf_op jit(solution)/shard_map/gather_rows/pallas_call | solution.py:202
  60.7 1.1 select_reduce_fusion
  61.8 0.1 mul.41
  61.9 0.0 copy-start.2
  61.9 0.0 copy-start.6
  61.9 5.3 %fusion.17 = f32[512,512]{1,0:T(8,128)S(1)} fusion(bf16[512,3584]{1,0:T(8,128)(2,1)} %bitcast.54, bf16[3584,512]{1,0:T(8,128)(2,1)} %param.13), kind=kOutput, calls=%fused_computation.36 | convolution fusion | flops 1879048192 | bytes 8388608 | tf_op jit(solution)/shard_map/dot_general | solution.py:405
  67.3 0.0 copy-done.2
  67.3 0.0 copy-done.6
  67.3 0.0 copy-start.5
  67.3 0.0 copy-start.8
  67.3 2.1 %fusion.18 = f32[512,512]{1,0:T(8,128)S(1)} fusion(bf16[512,3584]{1,0:T(8,128)(2,1)S(1)} %bitcast.55, bf16[3584,512]{1,0:T(8,128)(2,1)S(1)} %copy-done.2), kind=kOutput, calls=%fused_computation.37 | convolution fusion | flops 1879048192 | bytes 8388608 | tf_op jit(solution)/shard_map/dot_general | solution.py:406
  69.4 0.0 copy-done.5
  69.4 1.1 copy-done.8
  70.5 0.0 copy-start.3
  70.5 2.5 %multiply_convert_fusion = (bf16[512,512]{1,0:T(8,128)(2,1)S(1)}, bf16[512,512]{1,0:T(8,128)(2,1)S(1)}, bf16[512,512]{1,0:T(8,128)(2,1)S(1)}) fusion(f32[512,512]{1,0:T(8,128)S(1)} %fusion.17, f32[512,512]{1,0:T(8,128)S(1)} %fusion.18, f32[512]{0:T(512)S(1)} %mul.41, bf16[512,3584]{1,0:T(8,128)(2,1)S(1)} %bitcast.59, bf16[3584,512]{1,0:T(8,128)(2,1)S(1)} %copy-done.5), kind=kOutput, calls=%fused_computation.13 | convolution fusion | flops 1883504640 | bytes 11012096 | tf_op jit(solution)/shard_map/dot_general | solution.py:410
  72.9 0.0 copy-start.4
  73.0 0.2 pad_maximum_fusion.acts
  73.1 0.0 copy-done.3
  73.1 2.1 %fusion.19 = f32[512,3584]{1,0:T(8,128)S(1)} fusion(bf16[512,512]{1,0:T(8,128)(2,1)S(1)} %get-tuple-element.22, bf16[3584,512]{1,0:T(8,128)(2,1)S(1)} %copy-done.3), kind=kOutput, calls=%fused_computation.38 | convolution fusion | flops 1879048192 | bytes 11534336 | tf_op jit(solution)/shard_map/dot_general | solution.py:414
  75.3 2.1 %add_convert_fusion = bf16[512,3584]{1,0:T(8,128)(2,1)S(1)} fusion(f32[512,3584]{1,0:T(8,128)S(1)} %fusion.19, bf16[512,512]{1,0:T(8,128)(2,1)S(1)} %get-tuple-element.21, bf16[3584,512]{1,0:T(8,128)(2,1)S(1)} %copy-done.2), kind=kOutput, calls=%fused_computation | convolution fusion | flops 1882718208 | bytes 15204352 | tf_op jit(solution)/shard_map/dot_general | solution.py:415
  77.4 0.0 copy-done.4
  77.4 2.1 %convolution_convert_fusion = bf16[512,3584]{1,0:T(8,128)(2,1)S(1)} fusion(bf16[512,512]{1,0:T(8,128)(2,1)S(1)} %get-tuple-element.23, bf16[3584,512]{1,0:T(8,128)(2,1)S(1)} %copy-done.5), kind=kOutput, calls=%fused_computation.1 | convolution fusion | flops 1880883200 | bytes 7864320 | tf_op jit(solution)/shard_map/dot_general | solution.py:413
  79.5 54.7 %return_rows.1 = (bf16[32,3584]{1,0:T(8,128)(2,1)S(1)}, bf16[32,3584]{1,0:T(8,128)(2,1)S(1)}, bf16[3,512,512]{2,1,0:T(8,128)(2,1)S(1)}) custom-call(bf16[16,32,3584]{2,1,0:T(8,128)(2,1)S(1)} %bitcast.42, bf16[16,32,3584]{2,1,0:T(8,128)(2,1)S(1)} %bitcast.41, bf16[3,512,512]{2,1,0:T(8,128)(2,1)S(1)} %pad_maximum_fusion.acts), custom_call_target="tpu_custom_call" | custom-call | bytes 11927552 | tf_op jit(solution)/shard_map/return_rows/pallas_call | solution.py:338
  134.2 0.0 copy-start.1
  134.2 2.9 %fusion = f32[1792,512]{1,0:T(8,128)S(1)} fusion(bf16[512,512]{1,0:T(8,128)(2,1)} %copy-done.4, bf16[512,3584]{1,0:T(8,128)(2,1)} %bitcast.58, s32[]{:T(128)S(6)} %select_n.37), kind=kOutput, calls=%fused_computation.5 | convolution fusion | flops 939524096 | bytes 6029316 | tf_op jit(solution)/shard_map/dot_general | solution.py:424
  137.0 0.0 copy-done.1
  137.1 0.0 copy-start.7
  137.1 3.0 %convolution_add_fusion = f32[1792,512]{1,0:T(8,128)} fusion(f32[1792,512]{1,0:T(8,128)S(1)} %fusion, bf16[512,1792]{1,0:T(8,128)(2,1)S(1)} %bitcast.47, bf16[3,512,512]{2,1,0:T(8,128)(2,1)S(1)} %get-tuple-element.19), kind=kOutput, calls=%fused_computation.2 | convolution fusion | flops 940441600 | bytes 9699328 | tf_op jit(solution)/shard_map/dot_general | solution.py:425
  140.1 0.0 copy-done.7
  140.1 0.0 copy-start
  140.1 1.2 fusion.2
  141.3 0.3 copy-done
  141.6 3.0 %convolution_add_fusion.1 = f32[1792,512]{1,0:T(8,128)} fusion(f32[1792,512]{1,0:T(8,128)S(1)} %fusion.2, bf16[512,1792]{1,0:T(8,128)(2,1)S(1)} %bitcast.45, bf16[3,512,512]{2,1,0:T(8,128)(2,1)S(1)} %get-tuple-element.19), kind=kOutput, calls=%fused_computation.3 | convolution fusion | flops 940441600 | bytes 9699328 | tf_op jit(solution)/shard_map/dot_general | solution.py:425
  144.6 1.1 fusion.4
  145.8 3.0 %convolution_add_fusion.2 = f32[1792,512]{1,0:T(8,128)} fusion(f32[1792,512]{1,0:T(8,128)S(1)} %fusion.4, bf16[512,1792]{1,0:T(8,128)(2,1)S(1)} %bitcast.46, bf16[3,512,512]{2,1,0:T(8,128)(2,1)S(1)} %get-tuple-element.19), kind=kOutput, calls=%fused_computation.4 | convolution fusion | flops 940441600 | bytes 9699328 | tf_op jit(solution)/shard_map/dot_general | solution.py:425
  148.8 0.7 copy.19
  149.5 0.7 copy.20
  (2 shorter events, 0.0 us)
Async XLA Ops:
  61.9 5.4 %copy-start.2 = (bf16[3584,512]{1,0:T(8,128)(2,1)S(1)}, bf16[3584,512]{1,0:T(8,128)(2,1)}, u32[]{:S(2)}) copy-start(bf16[3584,512]{1,0:T(8,128)(2,1)} %param.14) | copy-start | bytes 11010052
  61.9 5.4 %copy-start.6 = (bf16[16,32,3584]{2,1,0:T(8,128)(2,1)S(1)}, bf16[16,32,3584]{2,1,0:T(8,128)(2,1)}, u32[]{:S(2)}) copy-start(bf16[16,32,3584]{2,1,0:T(8,128)(2,1)} %get-tuple-element.14) | copy-start | bytes 11010052
  67.3 2.1 %copy-start.5 = (bf16[3584,512]{1,0:T(8,128)(2,1)S(1)}, bf16[3584,512]{1,0:T(8,128)(2,1)}, u32[]{:S(2)}) copy-start(bf16[3584,512]{1,0:T(8,128)(2,1)} %param.15) | copy-start | bytes 11010052
  67.3 3.2 %copy-start.8 = (bf16[16,32,3584]{2,1,0:T(8,128)(2,1)S(1)}, bf16[16,32,3584]{2,1,0:T(8,128)(2,1)}, u32[]{:S(2)}) copy-start(bf16[16,32,3584]{2,1,0:T(8,128)(2,1)} %get-tuple-element.15) | copy-start | bytes 11010052
  70.5 2.7 %copy-start.3 = (bf16[3584,512]{1,0:T(8,128)(2,1)S(1)}, bf16[3584,512]{1,0:T(8,128)(2,1)}, u32[]{:S(2)}) copy-start(bf16[3584,512]{1,0:T(8,128)(2,1)} %param.13) | copy-start | bytes 11010052
  72.9 4.4 %copy-start.4 = (bf16[512,512]{1,0:T(8,128)(2,1)}, bf16[512,512]{1,0:T(8,128)(2,1)S(1)}, u32[]{:S(2)}) copy-start(bf16[512,512]{1,0:T(8,128)(2,1)S(1)} %get-tuple-element.23) | copy-start | bytes 1572868
  134.2 2.9 %copy-start.1 = (bf16[16,32,1792]{2,1,0:T(8,128)(2,1)S(1)}, bf16[16,32,1792]{2,1,0:T(8,128)(2,1)}, u32[]{:S(2)}) copy-start(bf16[16,32,1792]{2,1,0:T(8,128)(2,1)} %get-tuple-element.20) | copy-start | bytes 5505028
  137.1 3.0 %copy-start.7 = (bf16[16,32,3584]{2,1,0:T(8,128)(2,1)S(1)}, bf16[16,32,3584]{2,1,0:T(8,128)(2,1)}, u32[]{:S(2)}) copy-start(bf16[16,32,3584]{2,1,0:T(8,128)(2,1)} %get-tuple-element.14) | copy-start | bytes 11010052
  140.1 1.5 copy-start

commit v4 on v3

--- a/solution.py
+++ b/solution.py
@@ -45,19 +45,21 @@
 
 def gather_kernel(
     layers, t_ref, g_ref, w_ref, own_t, own_g, own_w, oth_t, oth_g,
-    local_sem, zs, zr, xs, xr, cs, cr, ys, yr, fs, fr,
+    local_sem, near_sem, zs, zr, xs, xr, cs, cr, ys, yr, fs, fr,
 ):
     half, layer, side, core = place(layers)
     me = block_of(layer, side, core)
-    width = oth_t.shape[2]
+    width = oth_t.shape[3]
     greet(layers, half, layer, side, core)
     own_in = (t_ref, g_ref, w_ref)
     own = (own_t, own_g, own_w)
-    oth = (oth_t, oth_g)
+    halves = (oth_t, oth_g)
+    oth = (oth_t.at[1], oth_g.at[1])
     across = (half, block_of(layer, 1 - side, core))
     sibling = (half, block_of(layer, side, 1 - core))
     partner = (1 - half, me)
     cols = pl.ds(pl.multiple_of((1 - half) * width, 128), width)
+    near = pl.ds(pl.multiple_of(half * width, 128), width)
     slots = 2 * layers - 1
     arrays = (2, 0, 1)
 
@@ -154,9 +156,14 @@
                 s = 1 - side if through else side
                 given(ok, lambda n=n, m=m, s=s, origin=origin, through=through: body(n, m, s, origin, through))
 
+    def keep(a, b, m, first):
+        src = own_in[a] if first else own[a].at[b]
+        return pltpu.make_async_copy(src.at[:, near], halves[a].at[0, b], near_sem.at[a, m])
+
     def pass_on(n, m, s, origin, through):
         b = block_of(origin, s, core)
         for a in range(2):
+            keep(a, b, m, n == 0 and not through).start()
             dst = oth[a].at[b]
             remote(dst, dst, ys.at[a, m], yr.at[a, m], partner).wait_recv()
             remote(dst, dst, fs.at[a, m], fr.at[a, m], sibling).start()
@@ -167,6 +174,7 @@
             dst = own[a].at[b]
             remote(dst, dst, cs.at[a, m], cr.at[a, m], sibling).wait_recv()
             if a < 2:
+                keep(a, b, m + 2 * slots, False).start()
                 dst = oth[a].at[b]
                 remote(dst, dst, fs.at[a, m], fr.at[a, m], sibling).wait_recv()
         mine = block_of(origin, s, core)
@@ -186,8 +194,14 @@
                             lambda a=a, up=up, step=step: along_copy(a, own[a].at[mine], mine, up, step).wait_send()
                         )
 
+    def settle(n, m, s, origin, through):
+        for a in range(2):
+            keep(a, block_of(origin, s, core), m, n == 0 and not through).wait()
+            keep(a, block_of(origin, s, 1 - core), m + 2 * slots, False).wait()
+
     each(pass_on)
     each(finish)
+    each(settle)
     for copy in locals_:
         copy.wait()
 
@@ -205,13 +219,14 @@
             jax.ShapeDtypeStruct((blocks, rows, width), tokens.dtype),
             jax.ShapeDtypeStruct((blocks, rows, width), cots.dtype),
             jax.ShapeDtypeStruct((blocks, rows, weights.shape[1]), weights.dtype),
-            jax.ShapeDtypeStruct((blocks, rows, width // 2), tokens.dtype),
-            jax.ShapeDtypeStruct((blocks, rows, width // 2), cots.dtype),
+            jax.ShapeDtypeStruct((2, blocks, rows, width // 2), tokens.dtype),
+            jax.ShapeDtypeStruct((2, blocks, rows, width // 2), cots.dtype),
         ),
         in_specs=[anywhere] * 3,
         out_specs=(anywhere,) * 5,
         scratch_shapes=[
             dma((3,)),
+            dma((2, 4 * slots)),
             dma((3, slots)), dma((3, slots)),
             dma((3, slots)), dma((3, slots)),
             dma((3, 2 * slots)), dma((3, 2 * slots)),
@@ -225,8 +240,8 @@
 
 
 def return_kernel(
-    layers, r0, r1, acts, out0, out1, oth_acts, mine, from_core, from_side, from_layer,
-    local_sem, cs, cr, xs, xr, zs, zr, hs, hr,
+    layers, r0, r1, a0, a1, a2, out0, out1, both0, both1, both2, mine, from_core, from_side, from_layer,
+    local_sem, near_sem, cs, cr, xs, xr, zs, zr, hs, hr,
 ):
     half, layer, side, core = place(layers)
     greet(layers, half, layer, side, core)
@@ -237,8 +252,10 @@
     partner = (1 - half, block_of(layer, side, core))
     parts = (r0, r1)
     outs = (out0, out1)
-    swap = remote(acts, oth_acts, hs, hr, partner)
-    swap.start()
+    acts = (a0, a1, a2)
+    both = (both0, both1, both2)
+    swaps = [remote(acts[n], both[n].at[1], hs.at[n], hr.at[n], partner) for n in range(3)]
+    stays = [pltpu.make_async_copy(acts[n], both[n].at[0], near_sem.at[n]) for n in range(3)]
     core_in = {}
     local_in = {}
     for k in range(layers):
@@ -301,6 +318,8 @@
     for k, a in units[:window]:
         first(k, a)
         side_in[a, k].start()
+    for copy in swaps + stays:
+        copy.start()
     for u, (k, a) in enumerate(units):
         later = units[u + window] if u + window < len(units) else None
         if later is not None:
@@ -322,7 +341,8 @@
             outs[a][:, c] = total.astype(outs[a].dtype)
 
         chunks(body)
-    swap.wait()
+    for copy in swaps + stays:
+        copy.wait()
     for copies in (core_in, side_in, layer_in):
         for copy in copies.values():
             copy.wait_send()
@@ -340,27 +360,27 @@
         out_shape=(
             jax.ShapeDtypeStruct((rows, width), kind),
             jax.ShapeDtypeStruct((rows, width), kind),
-            jax.ShapeDtypeStruct(acts.shape, acts.dtype),
-        ),
-        in_specs=[anywhere] * 3,
-        out_specs=(whole, whole, anywhere),
+        ) + tuple(jax.ShapeDtypeStruct((2,) + act.shape, act.dtype) for act in acts),
+        in_specs=[anywhere] * 5,
+        out_specs=(whole, whole) + (anywhere,) * 3,
         scratch_shapes=[
             pltpu.VMEM((2, 2 * layers, rows, width), kind),
             pltpu.VMEM((2, 2 * layers, rows, width), kind),
             pltpu.VMEM((2, layers, rows, width), kind),
             pltpu.VMEM((2, layers - 1, rows, width), kind),
             dma((2, 2 * layers)),
+            dma((3,)),
             dma((2, 2 * layers)), dma((2, 2 * layers)),
             dma((2, layers)), dma((2, layers)),
             dma((2, layers - 1)), dma((2, layers - 1)),
-            dma, dma,
+            dma((3,)), dma((3,)),
         ],
         compiler_params=pltpu.CompilerParams(
             collective_id=1, has_side_effects=True, vmem_limit_bytes=min(need + (4 << 20), 60 << 20)
         ),
         cost_estimate=pl.CostEstimate(flops=0, bytes_accessed=need, transcendentals=0),
         name="return_rows",
-    )(part_out, part_dx, acts)
+    )(part_out, part_dx, *acts)
 
 
 def dense_weights(expert_ids, probs, marks, experts, capacity):
@@ -384,20 +404,19 @@
     width = tokens.shape[2]
     rows = 2 * tok_rows
     capacity = max(1, tok_rows * topk // experts)
-    half = lax.axis_index("dp")
     expert = lax.axis_index("expert") // SPLIT
     f32 = jnp.float32
     bf16 = jnp.bfloat16
     weights = dense_weights(expert_ids, route_probs, copy_marks, experts, capacity).reshape(rows, experts)
     lanes = -(-experts // 128) * 128
     weights = jnp.pad(weights, ((0, 0), (0, lanes - experts)))
-    own_t, own_g, own_w, oth_t, oth_g = gather(
+    own_t, own_g, own_w, both_t, both_g = gather(
         layers, tokens.reshape(rows, width), out_grad.reshape(rows, width), weights
     )
     own_t = own_t.reshape(-1, width)
     own_g = own_g.reshape(-1, width)
-    oth_t = oth_t.reshape(-1, width // 2)
-    oth_g = oth_g.reshape(-1, width // 2)
+    both_t = both_t.reshape(-1, width // 2)
+    both_g = both_g.reshape(-1, width // 2)
     mine = jnp.arange(lanes, dtype=jnp.int32) == expert
     p = jnp.sum(jnp.where(mine, own_w.reshape(-1, lanes), 0.0), axis=1, keepdims=True)
     contract = (((1,), (1,)), ((), ()))
@@ -413,23 +432,21 @@
     part_out = lax.dot_general(hidden, w_down, contract, preferred_element_type=f32).astype(bf16)
     part_dx = lax.dot_general(gate_grad, w_gate, contract, preferred_element_type=f32)
     part_dx = (part_dx + lax.dot_general(up_grad, w_up, contract, preferred_element_type=f32)).astype(bf16)
-    acts = jnp.stack([gate_grad, up_grad, hidden])
-    moe, grad_in, oth_acts = give_back(
-        layers, part_out.reshape(-1, rows, width), part_dx.reshape(-1, rows, width), acts
+    moe, grad_in, *acts = give_back(
+        layers, part_out.reshape(-1, rows, width), part_dx.reshape(-1, rows, width), (gate_grad, up_grad, hidden)
     )
-    my_t = lax.dynamic_slice_in_dim(own_t, half * (width // 2), width // 2, 1)
-    my_g = lax.dynamic_slice_in_dim(own_g, half * (width // 2), width // 2, 1)
-
-    def outer(near, near_act, far, far_act):
-        total = lax.dot_general(near, near_act, rows_first, preferred_element_type=f32)
-        return total + lax.dot_general(far, far_act, rows_first, preferred_element_type=f32)
+
+    def outer(rows_in, act):
+        return lax.dot_general(
+            rows_in, act.reshape(-1, act.shape[2]), rows_first, preferred_element_type=f32
+        )
 
     return (
         moe.reshape(tokens.shape),
         grad_in.reshape(tokens.shape),
-        outer(my_t, gate_grad, oth_t, oth_acts[0]),
-        outer(my_t, up_grad, oth_t, oth_acts[1]),
-        outer(my_g, hidden, oth_g, oth_acts[2]),
+        outer(both_t, acts[0]),
+        outer(both_t, acts[1]),
+        outer(both_g, acts[2]),
     )
 
 

time: 150 us -> 253 us (1.69)
  Pallas kernels: 111 us -> 216 us
    pallas_call x1, Pallas kernels: 56.5 us -> 163 us  [gather(): pl.pallas_call(functools.partial(gather_kernel, layers), out_shape=(jax.S...]
    dot_general x6 -> x3, matrix products: 14.3 us -> 11.9 us  [outer(): lax.dot_general(rows_in, act.reshape(-1, act.shape[2]), rows_first, prefe...]
where the time goes in v4:
time: 253 us; the launch traced here: 252 us
  Pallas kernels  216 us (85%)
  matrix products  28 us (11%)
  other arithmetic  3.9 us (2%)
  local copies, waits for them, and re-layouts  3.32 us (1%)
    pallas_call x1, Pallas kernels, gather(): pl.pallas_call(functools.partial(gather_kernel, layers), out_shape=(jax.S...  163 us
    pallas_call x1, Pallas kernels, give_back(): pl.pallas_call(functools.partial(return_kernel, layers), out_shape=(jax.S...  52.1 us
    dot_general x3, matrix products, outer(): lax.dot_general(rows_in, act.reshape(-1, act.shape[2]), rows_first, prefe...  11.9 us
    dot_general x1, matrix products, local(): gate_pre = jnp.dot(own_t, w_gate, preferred_element_type=f32)  5.35 us

profile of v4, /device:TPU:0, one launch (start us, length us, event | category | flops | bytes accessed | tf_op | source)
XLA Modules:
  0.0 251.6 jit_solution(16941132719855768632)
XLA Ops:
  0.7 0.7 fusion.1
  1.4 0.6 convert_reduce_fusion
  2.0 0.1 copy.15
  2.1 0.7 select_reduce_fusion.1
  2.8 0.7 compare_select_fusion
  3.5 0.1 and_select_fusion
  3.5 0.1 copy.16
  3.6 0.6 pad.4.w_ref
  4.2 163.4 %gather_rows.1 = (bf16[16,32,3584]{2,1,0:T(8,128)(2,1)}, bf16[16,32,3584]{2,1,0:T(8,128)(2,1)}, f32[16,32,128]{2,1,0:T(8,128)}, bf16[2,16,32,1792]{3,2,1,0:T(8,128)(2,1)}, bf16[2,16,32,1792]{3,2,1,0:T(8,128)(2,1)}) custom-call(bf16[32,3584]{1,0:T(8,128)(2,1)} %bitcast.39, bf16[32,3584]{1,0:T(8,128)(2,1)} %bitcast.40, f32[32,128]{1,0:T(8,128)} %pad.4.w_ref), custom_call_target="tpu_custom_call" | custom-call | bytes 11010048 | tf_op jit(solution)/shard_map/gather_rows/pallas_call | solution.py:216
  167.6 1.1 select_reduce_fusion
  168.7 0.1 mul.37
  168.8 0.0 copy-start
  168.8 0.0 copy-start.6
  168.8 5.3 %fusion.2 = f32[512,512]{1,0:T(8,128)S(1)} fusion(bf16[512,3584]{1,0:T(8,128)(2,1)} %bitcast.46, bf16[3584,512]{1,0:T(8,128)(2,1)} %param.13), kind=kOutput, calls=%fused_computation.17 | convolution fusion | flops 1879048192 | bytes 8388608 | tf_op jit(solution)/shard_map/dot_general | solution.py:424
  174.1 0.0 copy-done
  174.1 0.0 copy-done.6
  174.2 0.0 copy-start.2
  174.2 0.0 copy-start.5
  174.2 2.1 fusion.3
  176.2 0.0 copy-done.2
  176.2 1.1 copy-done.5
  177.3 0.0 copy-start.1
  177.3 2.4 multiply_convert_fusion
  179.8 0.0 copy-done.1
  179.8 2.1 fusion.4
  181.9 2.1 add_convert_fusion
  184.0 2.1 convolution_convert_fusion
  186.1 0.0 copy-start.4
  186.1 52.1 %return_rows.1 = (bf16[32,3584]{1,0:T(8,128)(2,1)S(1)}, bf16[32,3584]{1,0:T(8,128)(2,1)S(1)}, bf16[2,512,512]{2,1,0:T(8,128)(2,1)S(1)}, bf16[2,512,512]{2,1,0:T(8,128)(2,1)S(1)}, bf16[2,512,512]{2,1,0:T(8,128)(2,1)S(1)}) custom-call(bf16[16,32,3584]{2,1,0:T(8,128)(2,1)S(1)} %bitcast.33, bf16[16,32,3584]{2,1,0:T(8,128)(2,1)S(1)} %bitcast.32, ...), custom_call_target="tpu_custom_call" | custom-call | bytes 11927552 | tf_op jit(solution)/shard_map/return_rows/pallas_call | solution.py:358
  238.3 0.0 copy-done.4
  238.3 0.0 copy-start.3
  238.3 3.9 %fusion.7 = f32[1792,512]{1,0:T(8,128)} fusion(bf16[1024,1792]{1,0:T(8,128)(2,1)S(1)} %bitcast.44, bf16[1024,512]{1,0:T(8,128)(2,1)S(1)} %bitcast.38), kind=kOutput, calls=%fused_computation.22 | convolution fusion | flops 1879048192 | bytes 8388608 | tf_op jit(solution)/shard_map/dot_general | solution.py:440
  242.2 0.0 copy-done.3
  242.2 4.0 %fusion.6 = f32[1792,512]{1,0:T(8,128)} fusion(bf16[1024,1792]{1,0:T(8,128)(2,1)S(1)} %bitcast.42, bf16[1024,512]{1,0:T(8,128)(2,1)S(1)} %bitcast.37), kind=kOutput, calls=%fused_computation.21 | convolution fusion | flops 1879048192 | bytes 8388608 | tf_op jit(solution)/shard_map/dot_general | solution.py:440
  246.2 4.0 %fusion.5 = f32[1792,512]{1,0:T(8,128)} fusion(bf16[1024,1792]{1,0:T(8,128)(2,1)S(1)} %bitcast.43, bf16[1024,512]{1,0:T(8,128)(2,1)S(1)} %bitcast.36), kind=kOutput, calls=%fused_computation.20 | convolution fusion | flops 1879048192 | bytes 8388608 | tf_op jit(solution)/shard_map/dot_general | solution.py:440
  250.2 0.7 copy.19
  250.9 0.7 copy.20
  (2 shorter events, 0.0 us)
Async XLA Ops:
  168.8 5.4 %copy-start = (bf16[3584,512]{1,0:T(8,128)(2,1)S(1)}, bf16[3584,512]{1,0:T(8,128)(2,1)}, u32[]{:S(2)}) copy-start(bf16[3584,512]{1,0:T(8,128)(2,1)} %param.14) | copy-start | bytes 11010052
  168.8 5.4 %copy-start.6 = (bf16[16,32,3584]{2,1,0:T(8,128)(2,1)S(1)}, bf16[16,32,3584]{2,1,0:T(8,128)(2,1)}, u32[]{:S(2)}) copy-start(bf16[16,32,3584]{2,1,0:T(8,128)(2,1)} %get-tuple-element.16) | copy-start | bytes 11010052
  174.2 2.1 copy-start.2
  174.2 3.2 %copy-start.5 = (bf16[16,32,3584]{2,1,0:T(8,128)(2,1)S(1)}, bf16[16,32,3584]{2,1,0:T(8,128)(2,1)}, u32[]{:S(2)}) copy-start(bf16[16,32,3584]{2,1,0:T(8,128)(2,1)} %get-tuple-element.17) | copy-start | bytes 11010052
  177.3 2.5 copy-start.1
  186.1 52.2 %copy-start.4 = (bf16[2,16,32,1792]{3,2,1,0:T(8,128)(2,1)S(1)}, bf16[2,16,32,1792]{3,2,1,0:T(8,128)(2,1)}, u32[]{:S(2)}) copy-start(bf16[2,16,32,1792]{3,2,1,0:T(8,128)(2,1)} %get-tuple-element.23) | copy-start | bytes 11010052
  238.3 3.9 %copy-start.3 = (bf16[2,16,32,1792]{3,2,1,0:T(8,128)(2,1)S(1)}, bf16[2,16,32,1792]{3,2,1,0:T(8,128)(2,1)}, u32[]{:S(2)}) copy-start(bf16[2,16,32,1792]{3,2,1,0:T(8,128)(2,1)} %get-tuple-element.20) | copy-start | bytes 11010052
